TPU v7x, 32 devices: a whole 2x2x4 slice. The times are simulated.
32 devices in a mesh: seq: 16 (over z, y, core), fsdp: 2 (over x).
Axes of the slice: x: 2, y: 2, z: 4, core: 2. Of those that a mesh axis runs over, the one named last changes fastest.
Arguments:
- dna_embed: bfloat16 [2, 4096, 1024], P('fsdp', 'seq'), may hold values from -60 to 60
- site_owner: int32 [2, 4096, 1], P('fsdp', 'seq'), may hold values from 0 to 15; in each aligned block of 256 rows (0 to 255, 256 to 511, ..., all dimensions but the last counted through in order) at most 32 rows name the same one
- site_row: int32 [2, 4096], P('fsdp', 'seq'), may hold values from 0 to 2047
- variant_table: bfloat16 [32768, 1024], P('seq'), may hold values from -6 to 6
- norm_gain: float32 [1024], replicated, may hold values from 0.1 to 1.9
- conv_weight: bfloat16 [7, 1024], replicated, may hold values from -2.390625 to 2.390625
- qkv_weight: bfloat16 [1024, 3072], P(None, 'fsdp'), may hold values from -4 to 4
- out_weight: bfloat16 [1024, 1024], P(None, 'fsdp'), may hold values from -0.1875 to 0.1875
- attn_gain: float32 [1024], replicated, may hold values from 0.1 to 1.9
Outputs:
- mixed: bfloat16 [2, 4096, 1024], P('fsdp', 'seq')
Inputs may be any that keep to these rules, and one draw needn't show every extreme that they name: `site_owner`: in each haplotype the 256 positions of one device name one site range at most 32 times, and some site range exactly 32 times.
All inputs are finite; a program needn't handle non-finite values.
Results may differ from a plain program's by a relative error of at most 0.0075.
The roundings to bfloat16 on the way count: a program that leaves them out, or rounds other values in their place, can miss the bound.
Values may be sent and summed in bfloat16 or wider, within the bound.
A program may use at most 128 MiB of HBM per device.

v0:
```python
import jax
import jax.numpy as jnp
from jax import lax
from jax.sharding import PartitionSpec as P

HEAD = 64
WINDOW = 2048


EPSILON = 1e-05


def shifted(value, axis, steps):
    count = lax.axis_size(axis)
    first, last = (max(0, -steps), min(count, count - steps))
    return lax.ppermute(value, axis, [(source, source + steps) for source in range(first, last)])


def rms_scale(values, gain):
    return values * lax.rsqrt(jnp.mean(values * values, axis=-1, keepdims=True) + EPSILON) * gain


def local(
    dna_embed,
    site_owner,
    site_row,
    variant_table,
    norm_gain,
    conv_weight,
    qkv_weight,
    out_weight,
    attn_gain,
):
    seq_rank = lax.axis_index("seq")
    seq_count = lax.axis_size("seq")
    tok_rows = dna_embed.shape[1]
    model_width = dna_embed.shape[2]
    slot_count = max(2, 2 * tok_rows // seq_count)
    owner_ids = site_owner[0, :, 0]
    wanted_rows = site_row[0]
    owner_onehot = (owner_ids[:, None] == jnp.arange(seq_count, dtype=jnp.int32)[None, :]).astype(
        jnp.int32
    )
    earlier_same = jnp.cumsum(owner_onehot, axis=0) - owner_onehot
    rank_within = jnp.sum(earlier_same * owner_onehot, axis=1)
    slot_index = owner_ids * slot_count + rank_within
    request_table = jnp.zeros((seq_count * slot_count,), jnp.int32).at[slot_index].set(wanted_rows)
    request_table = request_table.reshape(seq_count, slot_count)
    found = variant_table[
        lax.all_to_all(request_table, "seq", split_axis=0, concat_axis=0, tiled=True)
    ]
    fetched = lax.all_to_all(found, "seq", split_axis=0, concat_axis=0, tiled=True)
    site_embed = fetched.reshape(seq_count * slot_count, model_width)[slot_index]
    resid = dna_embed[0].astype(jnp.float32) + site_embed.astype(jnp.float32)
    normed = rms_scale(resid, norm_gain).astype(jnp.bfloat16)
    taps = conv_weight.shape[0]
    rim_rows = shifted(normed[tok_rows - (taps - 1) :], "seq", 1)
    padded = jnp.concatenate([rim_rows, normed], axis=0)
    conv_sum = jnp.zeros((tok_rows, model_width), jnp.float32)
    for tap in range(taps):
        conv_sum = conv_sum + conv_weight[tap].astype(jnp.float32) * padded[
            taps - 1 - tap : taps - 1 - tap + tok_rows
        ].astype(jnp.float32)
    conv_out = conv_sum.astype(jnp.bfloat16)
    full_qkv, full_out = (
        lax.all_gather(qkv_weight, "fsdp", axis=1, tiled=True),
        lax.all_gather(out_weight, "fsdp", axis=1, tiled=True),
    )
    qkv = jnp.dot(conv_out, full_qkv, preferred_element_type=jnp.float32).astype(jnp.bfloat16)
    query = qkv[:, :model_width]
    local_kv = qkv[:, model_width:]
    reach_count = WINDOW // tok_rows
    earlier = [shifted(conv_out, "seq", reach_count - offset) for offset in range(reach_count)]
    past_conv = jnp.concatenate(earlier, axis=0)
    past_kv = jnp.dot(
        past_conv, full_qkv[:, model_width:], preferred_element_type=jnp.float32
    ).astype(jnp.bfloat16)
    keys_all = jnp.concatenate([past_kv, local_kv], axis=0)
    key_total = keys_all.shape[0]
    q_where = seq_rank * tok_rows + jnp.arange(tok_rows, dtype=jnp.int32)
    k_where = seq_rank * tok_rows - reach_count * tok_rows + jnp.arange(key_total, dtype=jnp.int32)
    allowed = (
        (k_where[None, :] <= q_where[:, None])
        & (k_where[None, :] > q_where[:, None] - WINDOW)
        & (k_where[None, :] >= 0)
    )
    head_count = model_width // HEAD
    group_heads = min(4, head_count)
    group_count = head_count // group_heads
    span = group_heads * HEAD

    def head_group(group_index):
        first_col = group_index * span
        q_group = lax.dynamic_slice_in_dim(query, first_col, span, 1).reshape(
            tok_rows, group_heads, HEAD
        )
        k_group = lax.dynamic_slice_in_dim(keys_all, first_col, span, 1).reshape(
            key_total, group_heads, HEAD
        )
        v_group = lax.dynamic_slice_in_dim(keys_all, model_width + first_col, span, 1).reshape(
            key_total, group_heads, HEAD
        )
        scores = jnp.einsum(
            "qhd,khd->hqk", q_group, k_group, preferred_element_type=jnp.float32
        ) * HEAD ** (-0.5)
        scores = jnp.where(allowed[None, :, :], scores, -jnp.inf)
        highest = jnp.max(scores, axis=-1, keepdims=True)
        expo = jnp.exp(scores - highest)
        probs = (expo / jnp.sum(expo, axis=-1, keepdims=True)).astype(jnp.bfloat16)
        attended = jnp.einsum("hqk,khd->qhd", probs, v_group, preferred_element_type=jnp.float32)
        return attended.reshape(tok_rows, span)

    grouped = lax.map(head_group, jnp.arange(group_count, dtype=jnp.int32))
    attended = jnp.moveaxis(grouped, 0, 1).reshape(tok_rows, model_width)
    attn_normed = rms_scale(attended, attn_gain).astype(jnp.bfloat16)
    mixed = jnp.dot(attn_normed, full_out, preferred_element_type=jnp.float32).astype(jnp.bfloat16)
    return mixed[None, :, :]


def solution(mesh):
    in_specs = (
        P("fsdp", "seq", None),
        P("fsdp", "seq", None),
        P("fsdp", "seq"),
        P("seq", None),
        P(),
        P(),
        P(None, "fsdp"),
        P(None, "fsdp"),
        P(),
    )
    out_specs = P("fsdp", "seq", None)
    return jax.shard_map(local, mesh=mesh, in_specs=in_specs, out_specs=out_specs, check_vma=False)
```

profile of v0, /device:TPU:18, one launch (start us, length us, event | category | flops | bytes accessed | tf_op | source)
XLA Modules:
  0.0 295.5 jit_solution(13186717767650903189)
XLA Ops:
  11.8 10.1 %all_to_all.17 = s32[16,1,32]{2,1,0:T(1,128)S(1)} all-to-all(s32[16,1,32]{2,1,0:T(1,128)S(1)} %all_to_all.11), channel_id=1, replica_groups=mesh['seq'=16,'fsdp'=2] {'seq'}, dimensions={0} | all-to-all | bytes 4096 | tf_op jit(solution)/shard_map/all_to_all | solution.py:50
  22.0 6.6 %gather_fusion = bf16[512,1024]{1,0:T(8,128)(2,1)} fusion(bf16[2048,1024]{1,0:T(8,128)(2,1)} %param.14, s32[1024]{0:T(1024)S(1)} %pad_clamp_fusion.1), kind=kCustom, calls=%fused_computation | custom fusion | bytes 2099200 | tf_op jit(solution)/shard_map/gather | solution.py:49
  28.6 6.0 %all-to-all-start.1 = ((bf16[16,32,1024]{2,1,0:T(8,128)(2,1)}), bf16[16,32,1024]{2,1,0:T(8,128)(2,1)S(1)}, u32[]{:S(2)}, u32[]{:S(2)}) async-start(bf16[16,32,1024]{2,1,0:T(8,128)(2,1)} %bitcast.10), calls=%async_computation.1 | async-start | bytes 2097152 | tf_op jit(solution)/shard_map/all_to_all | solution.py:52
  34.7 25.1 %all-to-all-done.1 = bf16[16,32,1024]{2,1,0:T(8,128)(2,1)S(1)} async-done(((bf16[16,32,1024]{2,1,0:T(8,128)(2,1)}), bf16[16,32,1024]{2,1,0:T(8,128)(2,1)S(1)}, u32[]{:S(2)}, u32[]{:S(2)}) %all-to-all-start.1) | async-done | bytes 1048608 | tf_op jit(solution)/shard_map/all_to_all | solution.py:52
  61.5 1.9 collective-permute-start
  63.5 4.0 %collective-permute-done = bf16[6,1024]{1,0:T(8,128)(2,1)S(1)} collective-permute-done((bf16[6,1024]{1,0:T(8,128)(2,1)S(1)}, bf16[6,1024]{1,0:T(8,128)(2,1)S(1)}, u32[]{:S(2)}, u32[]{:S(2)}) %collective-permute-start) | collective-permute-done | bytes 12320 | tf_op jit(solution)/shard_map/ppermute | solution.py:16
  69.7 1.9 collective-permute-start.2
  71.6 1.9 collective-permute-start.3
  73.6 1.9 collective-permute-start.4
  75.5 1.9 collective-permute-start.5
  77.5 8.6 %collective-permute-done.1 = bf16[256,1024]{1,0:T(8,128)(2,1)S(1)} collective-permute-done((bf16[256,1024]{1,0:T(8,128)(2,1)S(1)}, bf16[256,1024]{1,0:T(8,128)(2,1)S(1)}, u32[]{:S(2)}, u32[]{:S(2)}) %collective-permute-start.1) | collective-permute-done | bytes 524320 | tf_op jit(solution)/shard_map/ppermute | solution.py:16
  89.5 16.4 %collective-permute-start.7 = (bf16[256,1024]{1,0:T(8,128)(2,1)S(1)}, bf16[256,1024]{1,0:T(8,128)(2,1)S(1)}, u32[]{:S(2)}, u32[]{:S(2)}) collective-permute-start(bf16[256,1024]{1,0:T(8,128)(2,1)S(1)} %add_convert_fusion), channel_id=1, source_target_pairs={{0,4},{2,6},{4,8},{6,10},{8,12},{10,14},{12,16},{14,18},{16,20},{1... | collective-permute-start | bytes 1572872 | tf_op jit(solution)/shard_map/ppermute | solution.py:16
  106.8 5.0 %collective-permute-done.3 = bf16[256,1024]{1,0:T(8,128)(2,1)S(1)} collective-permute-done((bf16[256,1024]{1,0:T(8,128)(2,1)S(1)}, bf16[256,1024]{1,0:T(8,128)(2,1)S(1)}, u32[]{:S(2)}, u32[]{:S(2)}) %collective-permute-start.3) | collective-permute-done | bytes 524320 | tf_op jit(solution)/shard_map/ppermute | solution.py:16
  111.8 18.5 %collective-permute-start.8 = (bf16[256,1024]{1,0:T(8,128)(2,1)S(1)}, bf16[256,1024]{1,0:T(8,128)(2,1)S(1)}, u32[]{:S(2)}, u32[]{:S(2)}) collective-permute-start(bf16[256,1024]{1,0:T(8,128)(2,1)S(1)} %add_convert_fusion), channel_id=1, source_target_pairs={{0,2},{2,4},{4,6},{6,8},{8,10},{10,12},{12,14},{14,16},{16,18},{18... | collective-permute-start | bytes 1572872 | tf_op jit(solution)/shard_map/ppermute | solution.py:16
  131.9 12.2 %collective-permute-done.5 = bf16[256,1024]{1,0:T(8,128)(2,1)S(1)} collective-permute-done((bf16[256,1024]{1,0:T(8,128)(2,1)S(1)}, bf16[256,1024]{1,0:T(8,128)(2,1)S(1)}, u32[]{:S(2)}, u32[]{:S(2)}) %collective-permute-start.5) | collective-permute-done | bytes 524320 | tf_op jit(solution)/shard_map/ppermute | solution.py:16
  145.0 4.5 %collective-permute-done.6 = bf16[256,1024]{1,0:T(8,128)(2,1)S(1)} collective-permute-done((bf16[256,1024]{1,0:T(8,128)(2,1)S(1)}, bf16[256,1024]{1,0:T(8,128)(2,1)S(1)}, u32[]{:S(2)}, u32[]{:S(2)}) %collective-permute-start.6) | collective-permute-done | bytes 524320 | tf_op jit(solution)/shard_map/ppermute | solution.py:16
  150.4 38.0 %collective-permute-done.7 = bf16[256,1024]{1,0:T(8,128)(2,1)S(1)} collective-permute-done((bf16[256,1024]{1,0:T(8,128)(2,1)S(1)}, bf16[256,1024]{1,0:T(8,128)(2,1)S(1)}, u32[]{:S(2)}, u32[]{:S(2)}) %collective-permute-start.7) | collective-permute-done | bytes 524320 | tf_op jit(solution)/shard_map/ppermute | solution.py:16
  189.2 4.7 %collective-permute-done.8 = bf16[256,1024]{1,0:T(8,128)(2,1)S(1)} collective-permute-done((bf16[256,1024]{1,0:T(8,128)(2,1)S(1)}, bf16[256,1024]{1,0:T(8,128)(2,1)S(1)}, u32[]{:S(2)}, u32[]{:S(2)}) %collective-permute-start.8) | collective-permute-done | bytes 524320 | tf_op jit(solution)/shard_map/ppermute | solution.py:16
  194.7 4.7 %convolution_convert_fusion.1 = bf16[256,3072]{1,0:T(8,128)(2,1)S(1)} fusion(bf16[256,1024]{1,0:T(8,128)(2,1)S(1)} %add_convert_fusion, bf16[1024,3072]{1,0:T(8,128)(2,1)} %all-gather.3.cloned.1.call-done), kind=kOutput, calls=%fused_computation.26 | convolution fusion | flops 1611399168 | bytes 8388608 | tf_op jit(solution)/shard_map/dot_general | solution.py:69
  200.4 10.7 %convolution_convert_fusion = bf16[2048,2048]{1,0:T(8,128)(2,1)S(1)} fusion(bf16[2048,1024]{1,0:T(8,128)(2,1)} %constant_dynamic-update-slice_fusion.1, bf16[1024,3072]{1,0:T(8,128)(2,1)S(1)} %copy-done.4), kind=kOutput, calls=%fused_computation.24 | convolution fusion | flops 8594128896 | bytes 16777216 | tf_op jit(solution)/shard_map/dot_general | solution.py:75
  211.1 9.7 %pad_maximum_fusion = bf16[2304,2048]{1,0:T(8,128)(2,1)} fusion(bf16[256,2048]{1,0:T(8,128)(2,1)S(1)} %slice.93, bf16[2048,2048]{1,0:T(8,128)(2,1)S(1)} %convolution_convert_fusion), kind=kLoop, calls=%fused_computation.23 | loop fusion | flops 18874368 | bytes 18874368 | tf_op jit(solution)/shard_map/concatenate | solution.py:78
  220.7 12.2 %copy.13 = bf16[2304,2048]{0,1:T(8,128)(2,1)} copy(bf16[2304,2048]{1,0:T(8,128)(2,1)} %pad_maximum_fusion) | data formatting | bytes 18874368
  232.9 49.8 %while.13 = (s32[]{:T(128)}, f32[4,256,256]{1,2,0:T(8,128)}, s32[4]{0:T(128)S(1)}, bf16[2304,2048]{0,1:T(8,128)(2,1)}, bf16[256,1024]{1,0:T(8,128)(2,1)}, /*inde...) while((s32[]{:T(128)}, f32[4,256,256]{1,2,0:T(8,128)}, ...), condition=%wide.region_8.9_spmd.clone, body=%wide.region_5.8_spmd.clone.sunk | while | flops 929568256 | bytes 11622414 | solution.py:113
  237.6 3.5 %fusion.55 = f32[4,256]{1,0:T(4,128)S(1)} fusion(pred[256,2304]{1,0:T(8,128)(4,1)S(1)} %and_and_fusion.2, bf16[256,4,64]{0,2,1:T(8,128)(2,1)S(1)} %bitcast.99, bf16[2304,4,64]{0,2,1:T(8,128)(2,1)S(1)} %bitcast.94), kind=kOutput, calls=%fused_computation.89.clone.1 | convolution fusion | flops 311429376 | bytes 1904640 | tf_op jit(solution)/shard_map/while/body/eval_jaxpr/sub | solution.py:108
  241.2 3.5 %fusion.56 = f32[4,64,256]{2,1,0:T(8,128)S(1)} fusion(bf16[2304,4,64]{0,2,1:T(8,128)(2,1)S(1)} %bitcast.96, f32[4,256]{1,0:T(4,128)S(1)} %fusion.55, pred[256,2304]{1,0:T(8,128)(4,1)S(1)} %and_and_fusion.2, bf16[256,4,64]{0,2,1:T(8,128)(2,1)S(1)} %bitcast.100, bf16[2304,4,64]{0,2,1:T(8,128)(2,1)S(1)} %bitcast.95), kind=kOutput, calls=%fused_computation.12.clone.1 | convolution fusion | flops 615779584 | bytes 3346432 | tf_op jit(solution)/shard_map/while/body/eval_jaxpr/hqk,khd->qhd/dot_general | solution.py:110
  250.1 3.5 %fusion.55 = f32[4,256]{1,0:T(4,128)S(1)} fusion(pred[256,2304]{1,0:T(8,128)(4,1)S(1)} %and_and_fusion.2, bf16[256,4,64]{0,2,1:T(8,128)(2,1)S(1)} %bitcast.99, bf16[2304,4,64]{0,2,1:T(8,128)(2,1)S(1)} %bitcast.94), kind=kOutput, calls=%fused_computation.89.clone.1 | convolution fusion | flops 311429376 | bytes 1904640 | tf_op jit(solution)/shard_map/while/body/eval_jaxpr/sub | solution.py:108
  253.6 3.5 %fusion.56 = f32[4,64,256]{2,1,0:T(8,128)S(1)} fusion(bf16[2304,4,64]{0,2,1:T(8,128)(2,1)S(1)} %bitcast.96, f32[4,256]{1,0:T(4,128)S(1)} %fusion.55, pred[256,2304]{1,0:T(8,128)(4,1)S(1)} %and_and_fusion.2, bf16[256,4,64]{0,2,1:T(8,128)(2,1)S(1)} %bitcast.100, bf16[2304,4,64]{0,2,1:T(8,128)(2,1)S(1)} %bitcast.95), kind=kOutput, calls=%fused_computation.12.clone.1 | convolution fusion | flops 615779584 | bytes 3346432 | tf_op jit(solution)/shard_map/while/body/eval_jaxpr/hqk,khd->qhd/dot_general | solution.py:110
  262.5 3.5 %fusion.55 = f32[4,256]{1,0:T(4,128)S(1)} fusion(pred[256,2304]{1,0:T(8,128)(4,1)S(1)} %and_and_fusion.2, bf16[256,4,64]{0,2,1:T(8,128)(2,1)S(1)} %bitcast.99, bf16[2304,4,64]{0,2,1:T(8,128)(2,1)S(1)} %bitcast.94), kind=kOutput, calls=%fused_computation.89.clone.1 | convolution fusion | flops 311429376 | bytes 1904640 | tf_op jit(solution)/shard_map/while/body/eval_jaxpr/sub | solution.py:108
  266.0 3.5 %fusion.56 = f32[4,64,256]{2,1,0:T(8,128)S(1)} fusion(bf16[2304,4,64]{0,2,1:T(8,128)(2,1)S(1)} %bitcast.96, f32[4,256]{1,0:T(4,128)S(1)} %fusion.55, pred[256,2304]{1,0:T(8,128)(4,1)S(1)} %and_and_fusion.2, bf16[256,4,64]{0,2,1:T(8,128)(2,1)S(1)} %bitcast.100, bf16[2304,4,64]{0,2,1:T(8,128)(2,1)S(1)} %bitcast.95), kind=kOutput, calls=%fused_computation.12.clone.1 | convolution fusion | flops 615779584 | bytes 3346432 | tf_op jit(solution)/shard_map/while/body/eval_jaxpr/hqk,khd->qhd/dot_general | solution.py:110
  275.0 3.5 %fusion.55 = f32[4,256]{1,0:T(4,128)S(1)} fusion(pred[256,2304]{1,0:T(8,128)(4,1)S(1)} %and_and_fusion.2, bf16[256,4,64]{0,2,1:T(8,128)(2,1)S(1)} %bitcast.99, bf16[2304,4,64]{0,2,1:T(8,128)(2,1)S(1)} %bitcast.94), kind=kOutput, calls=%fused_computation.89.clone.1 | convolution fusion | flops 311429376 | bytes 1904640 | tf_op jit(solution)/shard_map/while/body/eval_jaxpr/sub | solution.py:108
  278.5 3.5 %fusion.56 = f32[4,64,256]{2,1,0:T(8,128)S(1)} fusion(bf16[2304,4,64]{0,2,1:T(8,128)(2,1)S(1)} %bitcast.96, f32[4,256]{1,0:T(4,128)S(1)} %fusion.55, pred[256,2304]{1,0:T(8,128)(4,1)S(1)} %and_and_fusion.2, bf16[256,4,64]{0,2,1:T(8,128)(2,1)S(1)} %bitcast.100, bf16[2304,4,64]{0,2,1:T(8,128)(2,1)S(1)} %bitcast.95), kind=kOutput, calls=%fused_computation.12.clone.1 | convolution fusion | flops 615779584 | bytes 3346432 | tf_op jit(solution)/shard_map/while/body/eval_jaxpr/hqk,khd->qhd/dot_general | solution.py:110
  285.6 3.1 %fusion.17 = bf16[1,256,1024]{2,1,0:T(8,128)(2,1)} fusion(bf16[256,1024]{0,1:T(8,128)(2,1)S(1)} %fusion.19, bf16[1024,1024]{1,0:T(8,128)(2,1)} %all-gather.5.cloned.1.call-done), kind=kOutput, calls=%fused_computation.33 | convolution fusion | flops 537133056 | bytes 3145728 | tf_op jit(solution)/shard_map/dot_general | solution.py:116
  (82 shorter events, 41.8 us)
Async XLA Ops:
  6.5 188.2 %all-gather.3.cloned.1.call-start = ((), (), s32[]{:S(2)}) async-start(), calls=%async_computation.2 | async-start | bytes 9437184 | tf_op jit(solution)/shard_map/all_gather | solution.py:66
  28.6 32.3 %copy-start = (bf16[1,256,1024]{2,1,0:T(8,128)(2,1)S(1)}, bf16[1,256,1024]{2,1,0:T(8,128)(2,1)}, u32[]{:S(2)}) copy-start(bf16[1,256,1024]{2,1,0:T(8,128)(2,1)} %param.11) | copy-start | bytes 1572868
  28.6 32.6 %copy-start.2 = (f32[1024]{0:T(1024)S(1)}, f32[1024]{0:T(1024)}, u32[]{:S(2)}) copy-start(f32[1024]{0:T(1024)} %param.15) | copy-start | bytes 12292
  28.6 31.2 %all-to-all-start.1 = ((bf16[16,32,1024]{2,1,0:T(8,128)(2,1)}), bf16[16,32,1024]{2,1,0:T(8,128)(2,1)S(1)}, u32[]{:S(2)}, u32[]{:S(2)}) async-start(bf16[16,32,1024]{2,1,0:T(8,128)(2,1)} %bitcast.10), calls=%async_computation.1 | async-start | bytes 2097152 | tf_op jit(solution)/shard_map/all_to_all | solution.py:52
  34.6 28.8 %copy-start.1 = (bf16[7,1024]{1,0:T(8,128)(2,1)S(1)}, bf16[7,1024]{1,0:T(8,128)(2,1)}, u32[]{:S(2)}) copy-start(bf16[7,1024]{1,0:T(8,128)(2,1)} %param.16) | copy-start | bytes 43012
  34.6 250.9 %all-gather.5.cloned.1.call-start = ((), (), s32[]{:S(2)}) async-start(), calls=%async_computation.3 | async-start | bytes 3145728 | tf_op jit(solution)/shard_map/all_gather | solution.py:67
  61.5 6.0 %collective-permute-start = (bf16[6,1024]{1,0:T(8,128)(2,1)S(1)}, bf16[6,1024]{1,0:T(8,128)(2,1)S(1)}, u32[]{:S(2)}, u32[]{:S(2)}) collective-permute-start(bf16[6,1024]{1,0:T(8,128)(2,1)S(1)} %slice.81), channel_id=1, source_target_pairs={{0,2},{2,4},{4,6},{6,8},{8,10},{10,12},{12,14},{14,16},{16,18},{18... | collective-permute-start | bytes 36872 | tf_op jit(solution)/shard_map/ppermute | solution.py:16
  68.4 17.7 %collective-permute-start.1 = (bf16[256,1024]{1,0:T(8,128)(2,1)S(1)}, bf16[256,1024]{1,0:T(8,128)(2,1)S(1)}, u32[]{:S(2)}, u32[]{:S(2)}) collective-permute-start(bf16[256,1024]{1,0:T(8,128)(2,1)S(1)} %add_convert_fusion), channel_id=1, source_target_pairs={{0,16},{2,18},{4,20},{6,22},{8,24},{10,26},{12,28},{14,30},{1,17},... | collective-permute-start | bytes 1572872 | tf_op jit(solution)/shard_map/ppermute | solution.py:16
  69.7 19.9 %collective-permute-start.2 = (bf16[256,1024]{1,0:T(8,128)(2,1)S(1)}, bf16[256,1024]{1,0:T(8,128)(2,1)S(1)}, u32[]{:S(2)}, u32[]{:S(2)}) collective-permute-start(bf16[256,1024]{1,0:T(8,128)(2,1)S(1)} %add_convert_fusion), channel_id=1, source_target_pairs={{0,14},{2,16},{4,18},{6,20},{8,22},{10,24},{12,26},{14,28},{16,30}... | collective-permute-start | bytes 1572872 | tf_op jit(solution)/shard_map/ppermute | solution.py:16
  71.6 40.1 %collective-permute-start.3 = (bf16[256,1024]{1,0:T(8,128)(2,1)S(1)}, bf16[256,1024]{1,0:T(8,128)(2,1)S(1)}, u32[]{:S(2)}, u32[]{:S(2)}) collective-permute-start(bf16[256,1024]{1,0:T(8,128)(2,1)S(1)} %add_convert_fusion), channel_id=1, source_target_pairs={{0,12},{2,14},{4,16},{6,18},{8,20},{10,22},{12,24},{14,26},{16,28}... | collective-permute-start | bytes 1572872 | tf_op jit(solution)/shard_map/ppermute | solution.py:16
  73.6 57.5 %collective-permute-start.4 = (bf16[256,1024]{1,0:T(8,128)(2,1)S(1)}, bf16[256,1024]{1,0:T(8,128)(2,1)S(1)}, u32[]{:S(2)}, u32[]{:S(2)}) collective-permute-start(bf16[256,1024]{1,0:T(8,128)(2,1)S(1)} %add_convert_fusion), channel_id=1, source_target_pairs={{0,10},{2,12},{4,14},{6,16},{8,18},{10,20},{12,22},{14,24},{16,26}... | collective-permute-start | bytes 1572872 | tf_op jit(solution)/shard_map/ppermute | solution.py:16
  75.5 68.6 %collective-permute-start.5 = (bf16[256,1024]{1,0:T(8,128)(2,1)S(1)}, bf16[256,1024]{1,0:T(8,128)(2,1)S(1)}, u32[]{:S(2)}, u32[]{:S(2)}) collective-permute-start(bf16[256,1024]{1,0:T(8,128)(2,1)S(1)} %add_convert_fusion), channel_id=1, source_target_pairs={{0,8},{2,10},{4,12},{6,14},{8,16},{10,18},{12,20},{14,22},{16,24},... | collective-permute-start | bytes 1572872 | tf_op jit(solution)/shard_map/ppermute | solution.py:16
  86.1 63.4 %collective-permute-start.6 = (bf16[256,1024]{1,0:T(8,128)(2,1)S(1)}, bf16[256,1024]{1,0:T(8,128)(2,1)S(1)}, u32[]{:S(2)}, u32[]{:S(2)}) collective-permute-start(bf16[256,1024]{1,0:T(8,128)(2,1)S(1)} %add_convert_fusion), channel_id=1, source_target_pairs={{0,6},{2,8},{4,10},{6,12},{8,14},{10,16},{12,18},{14,20},{16,22},{... | collective-permute-start | bytes 1572872 | tf_op jit(solution)/shard_map/ppermute | solution.py:16
  89.5 98.8 %collective-permute-start.7 = (bf16[256,1024]{1,0:T(8,128)(2,1)S(1)}, bf16[256,1024]{1,0:T(8,128)(2,1)S(1)}, u32[]{:S(2)}, u32[]{:S(2)}) collective-permute-start(bf16[256,1024]{1,0:T(8,128)(2,1)S(1)} %add_convert_fusion), channel_id=1, source_target_pairs={{0,4},{2,6},{4,8},{6,10},{8,12},{10,14},{12,16},{14,18},{16,20},{1... | collective-permute-start | bytes 1572872 | tf_op jit(solution)/shard_map/ppermute | solution.py:16
  111.8 82.1 %collective-permute-start.8 = (bf16[256,1024]{1,0:T(8,128)(2,1)S(1)}, bf16[256,1024]{1,0:T(8,128)(2,1)S(1)}, u32[]{:S(2)}, u32[]{:S(2)}) collective-permute-start(bf16[256,1024]{1,0:T(8,128)(2,1)S(1)} %add_convert_fusion), channel_id=1, source_target_pairs={{0,2},{2,4},{4,6},{6,8},{8,10},{10,12},{12,14},{14,16},{16,18},{18... | collective-permute-start | bytes 1572872 | tf_op jit(solution)/shard_map/ppermute | solution.py:16
  194.7 5.7 %copy-start.4 = (bf16[1024,3072]{1,0:T(8,128)(2,1)S(1)}, bf16[1024,3072]{1,0:T(8,128)(2,1)}, u32[]{:S(2)}) copy-start(bf16[1024,3072]{1,0:T(8,128)(2,1)} %all-gather.3.cloned.1.call-done) | copy-start | bytes 18874372
  232.9 51.2 %copy-start.3 = (f32[1024]{0:T(1024)S(1)}, f32[1024]{0:T(1024)}, u32[]{:S(2)}) copy-start(f32[1024]{0:T(1024)} %param.19) | copy-start | bytes 12292
Sparse Core Ops, SparseCore 0:
  8.9 80.4 all-gather.2
  91.0 33.1 all-gather.4
where the time goes:
time: 297 us; the launch traced here: 296 us
  waiting for transfers between devices  103 us (35%)
  starting transfers between devices  53.7 us (18%)
  matrix products  46.4 us (16%)
  local copies, waits for them, and re-layouts  46.2 us (16%)
  other arithmetic  19.3 us (6%)
  between operations  13.6 us (5%)
  blocking collectives  10.1 us (3%)
    ppermute x9, waiting for transfers between devices, shifted(): lax.ppermute(value, axis, [(source, source + steps) for source in range(f...  77.6 us
    ppermute x9, starting transfers between devices, shifted(): lax.ppermute(value, axis, [(source, source + steps) for source in range(f...  47.7 us
    all_to_all x1, waiting for transfers between devices, local(): lax.all_to_all(found, 'seq', split_axis=0, concat_axis=0, tiled=True)  25.1 us
    unnamed x18, local copies, waits for them, and re-layouts  18.2 us
    sub x4, matrix products, head_group(): expo = jnp.exp(scores - highest)  14 us
    dot_general x4, matrix products, head_group(): jnp.einsum('hqk,khd->qhd', probs, v_group, preferred_element_type=jnp.flo...  13.9 us
    dot_general x1, matrix products, local(): jnp.dot(past_conv, full_qkv[:, model_width:], preferred_element_type=jnp....  10.7 us
    all_to_all x1, blocking collectives, local(): lax.all_to_all(request_table, 'seq', split_axis=0, concat_axis=0, tiled=T...  10.1 us
  transfers between devices with their start and end apart: 12, of which 9 were waited for; matrix products, arithmetic and copies ran while one was open for 37% of the time, Pallas kernels for 0%

commit v1 on v0

--- a/solution.py
+++ b/solution.py
@@ -1,6 +1,10 @@
+import functools
+
 import jax
 import jax.numpy as jnp
 from jax import lax
+from jax.experimental import pallas as pl
+from jax.experimental.pallas import tpu as pltpu
 from jax.sharding import PartitionSpec as P
 
 HEAD = 64
@@ -67,54 +71,96 @@
         lax.all_gather(out_weight, "fsdp", axis=1, tiled=True),
     )
     qkv = jnp.dot(conv_out, full_qkv, preferred_element_type=jnp.float32).astype(jnp.bfloat16)
-    query = qkv[:, :model_width]
-    local_kv = qkv[:, model_width:]
     reach_count = WINDOW // tok_rows
     earlier = [shifted(conv_out, "seq", reach_count - offset) for offset in range(reach_count)]
     past_conv = jnp.concatenate(earlier, axis=0)
     past_kv = jnp.dot(
         past_conv, full_qkv[:, model_width:], preferred_element_type=jnp.float32
     ).astype(jnp.bfloat16)
-    keys_all = jnp.concatenate([past_kv, local_kv], axis=0)
-    key_total = keys_all.shape[0]
-    q_where = seq_rank * tok_rows + jnp.arange(tok_rows, dtype=jnp.int32)
-    k_where = seq_rank * tok_rows - reach_count * tok_rows + jnp.arange(key_total, dtype=jnp.int32)
-    allowed = (
-        (k_where[None, :] <= q_where[:, None])
-        & (k_where[None, :] > q_where[:, None] - WINDOW)
-        & (k_where[None, :] >= 0)
+    return attention(qkv, past_kv, full_out, attn_gain[None, :], tok_rows, model_width)[None, :, :]
+
+
+def attention_kernel(tok_rows, q_ref, kp_ref, vp_ref, kl_ref, vl_ref, out_w_ref, gain_ref, o_ref, att_ref):
+    pair = pl.program_id(0)
+    pairs = pl.num_programs(0)
+    rank = lax.axis_index("seq")
+    past = kp_ref.shape[0]
+    lanes = q_ref.shape[1]
+    low_half = lax.broadcasted_iota(jnp.int32, (tok_rows, lanes), 1) < HEAD
+    row = lax.broadcasted_iota(jnp.int32, (tok_rows, tok_rows), 0)
+    col = lax.broadcasted_iota(jnp.int32, (tok_rows, tok_rows), 1)
+    recent = col <= row
+    absent = past - rank * tok_rows
+    mid_col = tok_rows + lax.broadcasted_iota(jnp.int32, (tok_rows, past - tok_rows), 1)
+    query = q_ref[...]
+    scaled = query * jnp.asarray(HEAD ** (-0.5), query.dtype)
+    nt = (((1,), (1,)), ((), ()))
+    halves = []
+    for half in range(2):
+        keep = low_half if half == 0 else jnp.logical_not(low_half)
+        q_head = jnp.where(keep, scaled, jnp.zeros_like(scaled))
+        s_mid = lax.dot_general(q_head, kp_ref[tok_rows:, :], nt, preferred_element_type=jnp.float32)
+        s_old = lax.dot_general(q_head, kp_ref[:tok_rows, :], nt, preferred_element_type=jnp.float32)
+        s_new = lax.dot_general(q_head, kl_ref[...], nt, preferred_element_type=jnp.float32)
+        s_mid = jnp.where(mid_col >= absent, s_mid, -jnp.inf)
+        s_old = jnp.where(col >= absent, s_old, -jnp.inf)
+        s_edge = jnp.where(recent, s_new, s_old)
+        highest = jnp.maximum(
+            jnp.max(s_mid, axis=-1, keepdims=True), jnp.max(s_edge, axis=-1, keepdims=True)
+        )
+        e_mid = jnp.exp(s_mid - highest)
+        e_edge = jnp.exp(s_edge - highest)
+        total = jnp.sum(e_mid, axis=-1, keepdims=True) + jnp.sum(e_edge, axis=-1, keepdims=True)
+        inverse = 1.0 / total
+        p_mid = (e_mid * inverse).astype(jnp.bfloat16)
+        p_edge = e_edge * inverse
+        p_new = jnp.where(recent, p_edge, 0.0).astype(jnp.bfloat16)
+        p_old = jnp.where(recent, 0.0, p_edge).astype(jnp.bfloat16)
+        halves.append(
+            jnp.dot(p_mid, vp_ref[tok_rows:, :], preferred_element_type=jnp.float32)
+            + jnp.dot(p_old, vp_ref[:tok_rows, :], preferred_element_type=jnp.float32)
+            + jnp.dot(p_new, vl_ref[...], preferred_element_type=jnp.float32)
+        )
+    att_ref[:, pl.ds(pl.multiple_of(pair * lanes, lanes), lanes)] = jnp.where(
+        low_half, halves[0], halves[1]
     )
-    head_count = model_width // HEAD
-    group_heads = min(4, head_count)
-    group_count = head_count // group_heads
-    span = group_heads * HEAD
 
-    def head_group(group_index):
-        first_col = group_index * span
-        q_group = lax.dynamic_slice_in_dim(query, first_col, span, 1).reshape(
-            tok_rows, group_heads, HEAD
-        )
-        k_group = lax.dynamic_slice_in_dim(keys_all, first_col, span, 1).reshape(
-            key_total, group_heads, HEAD
-        )
-        v_group = lax.dynamic_slice_in_dim(keys_all, model_width + first_col, span, 1).reshape(
-            key_total, group_heads, HEAD
-        )
-        scores = jnp.einsum(
-            "qhd,khd->hqk", q_group, k_group, preferred_element_type=jnp.float32
-        ) * HEAD ** (-0.5)
-        scores = jnp.where(allowed[None, :, :], scores, -jnp.inf)
-        highest = jnp.max(scores, axis=-1, keepdims=True)
-        expo = jnp.exp(scores - highest)
-        probs = (expo / jnp.sum(expo, axis=-1, keepdims=True)).astype(jnp.bfloat16)
-        attended = jnp.einsum("hqk,khd->qhd", probs, v_group, preferred_element_type=jnp.float32)
-        return attended.reshape(tok_rows, span)
+    @pl.when(pair == pairs - 1)
+    def _():
+        attended = att_ref[...]
+        normed = rms_scale(attended, gain_ref[...]).astype(jnp.bfloat16)
+        o_ref[...] = jnp.dot(
+            normed, out_w_ref[...], preferred_element_type=jnp.float32
+        ).astype(o_ref.dtype)
 
-    grouped = lax.map(head_group, jnp.arange(group_count, dtype=jnp.int32))
-    attended = jnp.moveaxis(grouped, 0, 1).reshape(tok_rows, model_width)
-    attn_normed = rms_scale(attended, attn_gain).astype(jnp.bfloat16)
-    mixed = jnp.dot(attn_normed, full_out, preferred_element_type=jnp.float32).astype(jnp.bfloat16)
-    return mixed[None, :, :]
+
+def attention(qkv, past_kv, out_weight, gain, tok_rows, model_width):
+    lanes = 2 * HEAD
+    pairs = model_width // lanes
+    past = past_kv.shape[0]
+    return pl.pallas_call(
+        functools.partial(attention_kernel, tok_rows),
+        grid=(pairs,),
+        out_shape=jax.ShapeDtypeStruct((tok_rows, model_width), jnp.bfloat16),
+        in_specs=[
+            pl.BlockSpec((tok_rows, lanes), lambda h: (0, h)),
+            pl.BlockSpec((past, lanes), lambda h: (0, h)),
+            pl.BlockSpec((past, lanes), lambda h: (0, pairs + h)),
+            pl.BlockSpec((tok_rows, lanes), lambda h: (0, pairs + h)),
+            pl.BlockSpec((tok_rows, lanes), lambda h: (0, 2 * pairs + h)),
+            pl.BlockSpec(out_weight.shape, lambda h: (0, 0)),
+            pl.BlockSpec(gain.shape, lambda h: (0, 0)),
+        ],
+        out_specs=pl.BlockSpec((tok_rows, model_width), lambda h: (0, 0)),
+        scratch_shapes=[pltpu.VMEM((tok_rows, model_width), jnp.float32)],
+        compiler_params=pltpu.CompilerParams(vmem_limit_bytes=48 * 1024 * 1024),
+        cost_estimate=pl.CostEstimate(
+            flops=8 * tok_rows * (past + tok_rows) * model_width,
+            bytes_accessed=4 * past * model_width,
+            transcendentals=tok_rows * past * model_width // HEAD,
+        ),
+        name="window_attention",
+    )(qkv, past_kv, past_kv, qkv, qkv, out_weight, gain)
 
 
 def solution(mesh):

time: 297 us -> 245 us (0.82)
  local copies, waits for them, and re-layouts: 46.2 us -> 18 us
  matrix products: 46.4 us -> 18.2 us
  Pallas kernels: 0 us -> 23.5 us
  other arithmetic: 19.3 us -> 4.19 us
    pallas_call x0 -> x1, Pallas kernels: none -> 23.5 us  [attention(): pl.pallas_call(functools.partial(attention_kernel, tok_rows), grid=(pairs...]
    dot_general x5 -> x0, matrix products: 17 us -> none  [the longest x4 13.9 us: head_group(): jnp.einsum('hqk,khd->qhd', probs, v_group, preferred_element_type=jnp.flo...]
    sub x4 -> x0, matrix products: 14 us -> none  [head_group(): expo = jnp.exp(scores - highest)]
    dynamic_slice x16 -> x0, local copies, waits for them, and re-layouts: 13.7 us -> none  [the longest x4 7.14 us: head_group(): lax.dynamic_slice_in_dim(keys_all, first_col, span, 1)]
    unnamed x18 -> x19, local copies, waits for them, and re-layouts: 18.2 us -> 7.5 us
    concatenate x1 -> x0, other arithmetic: 9.65 us -> none  [local(): keys_all = jnp.concatenate([past_kv, local_kv], axis=0)]
  transfers between devices with their start and end apart: 12 -> 12, of which waited for: 9 -> 9; matrix products, arithmetic and copies ran while one was open for 37% -> 16% of each run, Pallas kernels for 0% -> 0%
where the time goes in v1:
time: 245 us
  waiting for transfers between devices  103 us (42%)
  starting transfers between devices  54 us (22%)
  Pallas kernels  23.5 us (10%)
  matrix products  18.2 us (7%)
  local copies, waits for them, and re-layouts  18 us (7%)
  between operations  13.6 us (6%)
  blocking collectives  10.1 us (4%)
  other arithmetic  4.19 us (2%)
    ppermute x9, waiting for transfers between devices, shifted(): lax.ppermute(value, axis, [(source, source + steps) for source in range(f...  77.5 us
    ppermute x9, starting transfers between devices, shifted(): lax.ppermute(value, axis, [(source, source + steps) for source in range(f...  47.9 us
    all_to_all x1, waiting for transfers between devices, local(): lax.all_to_all(found, 'seq', split_axis=0, concat_axis=0, tiled=True)  25.1 us
    pallas_call x1, Pallas kernels, attention(): pl.pallas_call(functools.partial(attention_kernel, tok_rows), grid=(pairs...  23.5 us
    dot_general x1, matrix products, local(): jnp.dot(past_conv, full_qkv[:, model_width:], preferred_element_type=jnp....  13.4 us
    all_to_all x1, blocking collectives, local(): lax.all_to_all(request_table, 'seq', split_axis=0, concat_axis=0, tiled=T...  10.1 us
    unnamed x19, local copies, waits for them, and re-layouts  7.5 us
    gather x1, local copies, waits for them, and re-layouts, local(): variant_table[lax.all_to_all(request_table, 'seq', split_axis=0, concat_a...  6.59 us
  transfers between devices with their start and end apart: 12, of which 9 were waited for; matrix products, arithmetic and copies ran while one was open for 16% of the time, Pallas kernels for 0%

profile of v1, /device:TPU:18, one launch (start us, length us, event | category | flops | bytes accessed | tf_op | source)
XLA Modules:
  0.0 244.8 jit_solution(867208694949048477)
XLA Ops:
  10.2 1.6 scatter_custom_fusion
  11.8 10.1 %all_to_all.17 = s32[16,1,32]{2,1,0:T(1,128)S(1)} all-to-all(s32[16,1,32]{2,1,0:T(1,128)S(1)} %all_to_all.11), channel_id=1, replica_groups=mesh['seq'=16,'fsdp'=2] {'seq'}, dimensions={0} | all-to-all | bytes 4096 | tf_op jit(solution)/shard_map/all_to_all | solution.py:54
  22.0 6.6 %gather_fusion = bf16[512,1024]{1,0:T(8,128)(2,1)} fusion(bf16[2048,1024]{1,0:T(8,128)(2,1)} %param.12, s32[1024]{0:T(1024)S(1)} %pad_clamp_fusion.1), kind=kCustom, calls=%fused_computation | custom fusion | bytes 2099200 | tf_op jit(solution)/shard_map/gather | solution.py:53
  28.6 6.0 %all-to-all-start.1 = ((bf16[16,32,1024]{2,1,0:T(8,128)(2,1)}), bf16[16,32,1024]{2,1,0:T(8,128)(2,1)S(1)}, u32[]{:S(2)}, u32[]{:S(2)}) async-start(bf16[16,32,1024]{2,1,0:T(8,128)(2,1)} %bitcast.10), calls=%async_computation.1 | async-start | bytes 2097152 | tf_op jit(solution)/shard_map/all_to_all | solution.py:56
  34.7 25.1 %all-to-all-done.1 = bf16[16,32,1024]{2,1,0:T(8,128)(2,1)S(1)} async-done(((bf16[16,32,1024]{2,1,0:T(8,128)(2,1)}), bf16[16,32,1024]{2,1,0:T(8,128)(2,1)S(1)}, u32[]{:S(2)}, u32[]{:S(2)}) %all-to-all-start.1) | async-done | bytes 1048608 | tf_op jit(solution)/shard_map/all_to_all | solution.py:56
  59.8 1.2 gather_fusion.1
  61.5 1.9 collective-permute-start
  63.4 4.0 %collective-permute-done = bf16[6,1024]{1,0:T(8,128)(2,1)S(1)} collective-permute-done((bf16[6,1024]{1,0:T(8,128)(2,1)S(1)}, bf16[6,1024]{1,0:T(8,128)(2,1)S(1)}, u32[]{:S(2)}, u32[]{:S(2)}) %collective-permute-start) | collective-permute-done | bytes 12320 | tf_op jit(solution)/shard_map/ppermute | solution.py:20
  67.4 0.9 add_convert_fusion
  68.3 1.3 collective-permute-start.1
  69.6 1.9 collective-permute-start.2
  71.6 1.9 collective-permute-start.3
  73.5 1.9 collective-permute-start.4
  75.4 1.9 collective-permute-start.5
  77.4 8.7 %collective-permute-done.1 = bf16[256,1024]{1,0:T(8,128)(2,1)S(1)} collective-permute-done((bf16[256,1024]{1,0:T(8,128)(2,1)S(1)}, bf16[256,1024]{1,0:T(8,128)(2,1)S(1)}, u32[]{:S(2)}, u32[]{:S(2)}) %collective-permute-start.1) | collective-permute-done | bytes 524320 | tf_op jit(solution)/shard_map/ppermute | solution.py:20
  86.1 1.9 collective-permute-start.6
  88.0 0.9 constant_dynamic-update-slice_fusion.7
  89.5 16.4 %collective-permute-start.7 = (bf16[256,1024]{1,0:T(8,128)(2,1)S(1)}, bf16[256,1024]{1,0:T(8,128)(2,1)S(1)}, u32[]{:S(2)}, u32[]{:S(2)}) collective-permute-start(bf16[256,1024]{1,0:T(8,128)(2,1)S(1)} %add_convert_fusion), channel_id=1, source_target_pairs={{0,4},{2,6},{4,8},{6,10},{8,12},{10,14},{12,16},{14,18},{16,20},{1... | collective-permute-start | bytes 1572872 | tf_op jit(solution)/shard_map/ppermute | solution.py:20
  106.0 0.9 constant_dynamic-update-slice_fusion.6
  106.8 4.9 %collective-permute-done.3 = bf16[256,1024]{1,0:T(8,128)(2,1)S(1)} collective-permute-done((bf16[256,1024]{1,0:T(8,128)(2,1)S(1)}, bf16[256,1024]{1,0:T(8,128)(2,1)S(1)}, u32[]{:S(2)}, u32[]{:S(2)}) %collective-permute-start.3) | collective-permute-done | bytes 524320 | tf_op jit(solution)/shard_map/ppermute | solution.py:20
  111.8 18.7 %collective-permute-start.8 = (bf16[256,1024]{1,0:T(8,128)(2,1)S(1)}, bf16[256,1024]{1,0:T(8,128)(2,1)S(1)}, u32[]{:S(2)}, u32[]{:S(2)}) collective-permute-start(bf16[256,1024]{1,0:T(8,128)(2,1)S(1)} %add_convert_fusion), channel_id=1, source_target_pairs={{0,2},{2,4},{4,6},{6,8},{8,10},{10,12},{12,14},{14,16},{16,18},{18... | collective-permute-start | bytes 1572872 | tf_op jit(solution)/shard_map/ppermute | solution.py:20
  132.1 12.0 %collective-permute-done.5 = bf16[256,1024]{1,0:T(8,128)(2,1)S(1)} collective-permute-done((bf16[256,1024]{1,0:T(8,128)(2,1)S(1)}, bf16[256,1024]{1,0:T(8,128)(2,1)S(1)}, u32[]{:S(2)}, u32[]{:S(2)}) %collective-permute-start.5) | collective-permute-done | bytes 524320 | tf_op jit(solution)/shard_map/ppermute | solution.py:20
  144.1 0.9 constant_dynamic-update-slice_fusion.3
  144.9 4.5 %collective-permute-done.6 = bf16[256,1024]{1,0:T(8,128)(2,1)S(1)} collective-permute-done((bf16[256,1024]{1,0:T(8,128)(2,1)S(1)}, bf16[256,1024]{1,0:T(8,128)(2,1)S(1)}, u32[]{:S(2)}, u32[]{:S(2)}) %collective-permute-start.6) | collective-permute-done | bytes 524320 | tf_op jit(solution)/shard_map/ppermute | solution.py:20
  149.5 0.8 constant_dynamic-update-slice_fusion.2
  150.3 38.0 %collective-permute-done.7 = bf16[256,1024]{1,0:T(8,128)(2,1)S(1)} collective-permute-done((bf16[256,1024]{1,0:T(8,128)(2,1)S(1)}, bf16[256,1024]{1,0:T(8,128)(2,1)S(1)}, u32[]{:S(2)}, u32[]{:S(2)}) %collective-permute-start.7) | collective-permute-done | bytes 524320 | tf_op jit(solution)/shard_map/ppermute | solution.py:20
  189.2 4.7 %collective-permute-done.8 = bf16[256,1024]{1,0:T(8,128)(2,1)S(1)} collective-permute-done((bf16[256,1024]{1,0:T(8,128)(2,1)S(1)}, bf16[256,1024]{1,0:T(8,128)(2,1)S(1)}, u32[]{:S(2)}, u32[]{:S(2)}) %collective-permute-start.8) | collective-permute-done | bytes 524320 | tf_op jit(solution)/shard_map/ppermute | solution.py:20
  193.9 0.8 constant_dynamic-update-slice_fusion
  194.7 4.7 %convolution_convert_fusion.1.q_ref.kl_ref.vl_ref = bf16[256,3072]{1,0:T(8,128)(2,1)S(1)} fusion(bf16[256,1024]{1,0:T(8,128)(2,1)S(1)} %add_convert_fusion, bf16[1024,3072]{1,0:T(8,128)(2,1)} %all-gather.3.cloned.1.call-done), kind=kOutput, calls=%fused_computation.5 | convolution fusion | flops 1611399168 | bytes 8388608 | tf_op jit(solution)/shard_map/dot_general | solution.py:73
  199.5 13.4 %convolution_convert_fusion.kp_ref.vp_ref = bf16[2048,2048]{1,0:T(8,128)(2,1)} fusion(bf16[2048,1024]{1,0:T(8,128)(2,1)} %constant_dynamic-update-slice_fusion, bf16[1024,3072]{1,0:T(8,128)(2,1)S(1)} %copy-done.5), kind=kOutput, calls=%fused_computation.3 | convolution fusion | flops 8594128896 | bytes 16777216 | tf_op jit(solution)/shard_map/dot_general | solution.py:77
  212.9 1.6 copy-done
  214.5 23.5 %window_attention.1 = bf16[256,1024]{1,0:T(8,128)(2,1)} custom-call(bf16[256,3072]{1,0:T(8,128)(2,1)S(1)} %convolution_convert_fusion.1.q_ref.kl_ref.vl_ref, bf16[2048,2048]{1,0:T(8,128)(2,1)} %convolution_convert_fusion.kp_ref.vp_ref, bf16[2048,2048]{1,0:T(8,128)(2,1)} %convolution_convert_fusion.kp_ref.vp_ref, ...), custom_call_target="tpu_custom_call" | custom-call | flops 4831838208 | bytes 8388608 | tf_op jit(solution)/shard_map/window_attention/pallas_call | solution.py:141
  (39 shorter events, 7.6 us)
Async XLA Ops:
  6.5 188.2 %all-gather.3.cloned.1.call-start = ((), (), s32[]{:S(2)}) async-start(), calls=%async_computation.2 | async-start | bytes 9437184 | tf_op jit(solution)/shard_map/all_gather | solution.py:70
  28.6 32.3 %copy-start.2 = (bf16[1,256,1024]{2,1,0:T(8,128)(2,1)S(1)}, bf16[1,256,1024]{2,1,0:T(8,128)(2,1)}, u32[]{:S(2)}) copy-start(bf16[1,256,1024]{2,1,0:T(8,128)(2,1)} %param.9) | copy-start | bytes 1572868
  28.6 32.6 %copy-start.4 = (f32[1024]{0:T(1024)S(1)}, f32[1024]{0:T(1024)}, u32[]{:S(2)}) copy-start(f32[1024]{0:T(1024)} %param.13) | copy-start | bytes 12292
  28.6 31.2 %all-to-all-start.1 = ((bf16[16,32,1024]{2,1,0:T(8,128)(2,1)}), bf16[16,32,1024]{2,1,0:T(8,128)(2,1)S(1)}, u32[]{:S(2)}, u32[]{:S(2)}) async-start(bf16[16,32,1024]{2,1,0:T(8,128)(2,1)} %bitcast.10), calls=%async_computation.1 | async-start | bytes 2097152 | tf_op jit(solution)/shard_map/all_to_all | solution.py:56
  34.6 28.8 %copy-start.3 = (bf16[7,1024]{1,0:T(8,128)(2,1)S(1)}, bf16[7,1024]{1,0:T(8,128)(2,1)}, u32[]{:S(2)}) copy-start(bf16[7,1024]{1,0:T(8,128)(2,1)} %param.14) | copy-start | bytes 43012
  34.6 178.3 %all-gather.5.cloned.1.call-start = ((), (), s32[]{:S(2)}) async-start(), calls=%async_computation.3 | async-start | bytes 3145728 | tf_op jit(solution)/shard_map/all_gather | solution.py:71
  61.5 6.0 %collective-permute-start = (bf16[6,1024]{1,0:T(8,128)(2,1)S(1)}, bf16[6,1024]{1,0:T(8,128)(2,1)S(1)}, u32[]{:S(2)}, u32[]{:S(2)}) collective-permute-start(bf16[6,1024]{1,0:T(8,128)(2,1)S(1)} %slice.73), channel_id=1, source_target_pairs={{0,2},{2,4},{4,6},{6,8},{8,10},{10,12},{12,14},{14,16},{16,18},{18... | collective-permute-start | bytes 36872 | tf_op jit(solution)/shard_map/ppermute | solution.py:20
  68.3 17.7 %collective-permute-start.1 = (bf16[256,1024]{1,0:T(8,128)(2,1)S(1)}, bf16[256,1024]{1,0:T(8,128)(2,1)S(1)}, u32[]{:S(2)}, u32[]{:S(2)}) collective-permute-start(bf16[256,1024]{1,0:T(8,128)(2,1)S(1)} %add_convert_fusion), channel_id=1, source_target_pairs={{0,16},{2,18},{4,20},{6,22},{8,24},{10,26},{12,28},{14,30},{1,17},... | collective-permute-start | bytes 1572872 | tf_op jit(solution)/shard_map/ppermute | solution.py:20
  69.6 19.9 %collective-permute-start.2 = (bf16[256,1024]{1,0:T(8,128)(2,1)S(1)}, bf16[256,1024]{1,0:T(8,128)(2,1)S(1)}, u32[]{:S(2)}, u32[]{:S(2)}) collective-permute-start(bf16[256,1024]{1,0:T(8,128)(2,1)S(1)} %add_convert_fusion), channel_id=1, source_target_pairs={{0,14},{2,16},{4,18},{6,20},{8,22},{10,24},{12,26},{14,28},{16,30}... | collective-permute-start | bytes 1572872 | tf_op jit(solution)/shard_map/ppermute | solution.py:20
  71.6 40.2 %collective-permute-start.3 = (bf16[256,1024]{1,0:T(8,128)(2,1)S(1)}, bf16[256,1024]{1,0:T(8,128)(2,1)S(1)}, u32[]{:S(2)}, u32[]{:S(2)}) collective-permute-start(bf16[256,1024]{1,0:T(8,128)(2,1)S(1)} %add_convert_fusion), channel_id=1, source_target_pairs={{0,12},{2,14},{4,16},{6,18},{8,20},{10,22},{12,24},{14,26},{16,28}... | collective-permute-start | bytes 1572872 | tf_op jit(solution)/shard_map/ppermute | solution.py:20
  73.5 57.8 %collective-permute-start.4 = (bf16[256,1024]{1,0:T(8,128)(2,1)S(1)}, bf16[256,1024]{1,0:T(8,128)(2,1)S(1)}, u32[]{:S(2)}, u32[]{:S(2)}) collective-permute-start(bf16[256,1024]{1,0:T(8,128)(2,1)S(1)} %add_convert_fusion), channel_id=1, source_target_pairs={{0,10},{2,12},{4,14},{6,16},{8,18},{10,20},{12,22},{14,24},{16,26}... | collective-permute-start | bytes 1572872 | tf_op jit(solution)/shard_map/ppermute | solution.py:20
  75.4 68.7 %collective-permute-start.5 = (bf16[256,1024]{1,0:T(8,128)(2,1)S(1)}, bf16[256,1024]{1,0:T(8,128)(2,1)S(1)}, u32[]{:S(2)}, u32[]{:S(2)}) collective-permute-start(bf16[256,1024]{1,0:T(8,128)(2,1)S(1)} %add_convert_fusion), channel_id=1, source_target_pairs={{0,8},{2,10},{4,12},{6,14},{8,16},{10,18},{12,20},{14,22},{16,24},... | collective-permute-start | bytes 1572872 | tf_op jit(solution)/shard_map/ppermute | solution.py:20
  86.1 63.4 %collective-permute-start.6 = (bf16[256,1024]{1,0:T(8,128)(2,1)S(1)}, bf16[256,1024]{1,0:T(8,128)(2,1)S(1)}, u32[]{:S(2)}, u32[]{:S(2)}) collective-permute-start(bf16[256,1024]{1,0:T(8,128)(2,1)S(1)} %add_convert_fusion), channel_id=1, source_target_pairs={{0,6},{2,8},{4,10},{6,12},{8,14},{10,16},{12,18},{14,20},{16,22},{... | collective-permute-start | bytes 1572872 | tf_op jit(solution)/shard_map/ppermute | solution.py:20
  89.5 98.8 %collective-permute-start.7 = (bf16[256,1024]{1,0:T(8,128)(2,1)S(1)}, bf16[256,1024]{1,0:T(8,128)(2,1)S(1)}, u32[]{:S(2)}, u32[]{:S(2)}) collective-permute-start(bf16[256,1024]{1,0:T(8,128)(2,1)S(1)} %add_convert_fusion), channel_id=1, source_target_pairs={{0,4},{2,6},{4,8},{6,10},{8,12},{10,14},{12,16},{14,18},{16,20},{1... | collective-permute-start | bytes 1572872 | tf_op jit(solution)/shard_map/ppermute | solution.py:20
  111.8 82.1 %collective-permute-start.8 = (bf16[256,1024]{1,0:T(8,128)(2,1)S(1)}, bf16[256,1024]{1,0:T(8,128)(2,1)S(1)}, u32[]{:S(2)}, u32[]{:S(2)}) collective-permute-start(bf16[256,1024]{1,0:T(8,128)(2,1)S(1)} %add_convert_fusion), channel_id=1, source_target_pairs={{0,2},{2,4},{4,6},{6,8},{8,10},{10,12},{12,14},{14,16},{16,18},{18... | collective-permute-start | bytes 1572872 | tf_op jit(solution)/shard_map/ppermute | solution.py:20
  194.7 4.7 %copy-start.5 = (bf16[1024,3072]{1,0:T(8,128)(2,1)S(1)}, bf16[1024,3072]{1,0:T(8,128)(2,1)}, u32[]{:S(2)}) copy-start(bf16[1024,3072]{1,0:T(8,128)(2,1)} %all-gather.3.cloned.1.call-done) | copy-start | bytes 18874372
  199.4 13.4 %copy-start.1 = (f32[1024]{0:T(1024)S(1)}, f32[1024]{0:T(1024)}, u32[]{:S(2)}) copy-start(f32[1024]{0:T(1024)} %param.17) | copy-start | bytes 12292
  212.9 1.6 copy-start
Sparse Core Ops, SparseCore 0:
  8.9 80.4 all-gather.2
  91.0 33.1 all-gather.4

commit v2 on v1

--- a/solution.py
+++ b/solution.py
@@ -70,21 +70,118 @@
         lax.all_gather(qkv_weight, "fsdp", axis=1, tiled=True),
         lax.all_gather(out_weight, "fsdp", axis=1, tiled=True),
     )
-    qkv = jnp.dot(conv_out, full_qkv, preferred_element_type=jnp.float32).astype(jnp.bfloat16)
-    reach_count = WINDOW // tok_rows
-    earlier = [shifted(conv_out, "seq", reach_count - offset) for offset in range(reach_count)]
-    past_conv = jnp.concatenate(earlier, axis=0)
-    past_kv = jnp.dot(
-        past_conv, full_qkv[:, model_width:], preferred_element_type=jnp.float32
+    window = gather_window(conv_out)
+    query = jnp.dot(
+        conv_out, full_qkv[:, :model_width], preferred_element_type=jnp.float32
     ).astype(jnp.bfloat16)
-    return attention(qkv, past_kv, full_out, attn_gain[None, :], tok_rows, model_width)[None, :, :]
-
-
-def attention_kernel(tok_rows, q_ref, kp_ref, vp_ref, kl_ref, vl_ref, out_w_ref, gain_ref, o_ref, att_ref):
+    key_value = jnp.dot(
+        window, full_qkv[:, model_width:], preferred_element_type=jnp.float32
+    ).astype(jnp.bfloat16)
+    return attention(query, key_value, full_out, attn_gain[None, :], tok_rows, model_width)[None, :, :]
+
+
+MESH = pl.DeviceIdType.MESH
+CHUNKS = 4
+REACH_CHIPS = 4
+
+
+def window_kernel(count, conv_ref, win_ref, send_sem, recv_sem):
+    me = lax.axis_index("seq")
+    rows = conv_ref.shape[0]
+    part = rows // CHUNKS
+    core = lax.rem(me, 2)
+    odd = lax.rem(me // 2, 2)
+    ahead = lax.rem(me + 4, count)
+    behind = lax.rem(me + count - 4, count)
+    beside = me + 2 - 4 * odd
+    twin = me + 1 - 2 * core
+
+    def slot(back, chunk):
+        first = ((REACH_CHIPS - back) * 2 + core) * rows + chunk * part
+        return win_ref.at[pl.ds(pl.multiple_of(first, part), part)]
+
+    own = pl.multiple_of((REACH_CHIPS * 2 + core) * rows, rows)
+    win_ref[pl.ds(own, rows), :] = conv_ref[...]
+
+    barrier = pltpu.get_barrier_semaphore()
+    for other in (ahead, behind, beside, twin):
+        pl.semaphore_signal(barrier, inc=1, device_id={"seq": other}, device_id_type=MESH)
+    pl.semaphore_wait(barrier, 4)
+
+    def message(kind, chunk, source_back, target_back, target):
+        return pltpu.make_async_remote_copy(
+            src_ref=slot(source_back, chunk),
+            dst_ref=slot(target_back, chunk),
+            send_sem=send_sem.at[kind, chunk],
+            recv_sem=recv_sem.at[kind, chunk],
+            device_id={"seq": target},
+            device_id_type=MESH,
+        )
+
+    chunks = range(CHUNKS)
+    two = [message(0, j, 0, 2, ahead) for j in chunks]
+    four = [message(1, j, 2, 4, ahead) for j in chunks]
+    one = [message(2, j, 2 * odd, 1, beside) for j in chunks]
+    three = [message(3, j, 2 + 2 * odd, 3, beside) for j in chunks]
+    share = [[message(4 + back, j, back, back, twin) for j in chunks] for back in range(5)]
+    for j in chunks:
+        two[j].start()
+    for j in chunks:
+        share[0][j].start()
+    for j in chunks:
+        two[j].wait_recv()
+        four[j].start()
+        one[j].start()
+        share[2][j].start()
+    for j in chunks:
+        four[j].wait_recv()
+        three[j].start()
+        share[4][j].start()
+        one[j].wait_recv()
+        share[1][j].start()
+    for j in chunks:
+        three[j].wait_recv()
+        share[3][j].start()
+    for back in range(5):
+        for j in chunks:
+            share[back][j].wait_recv()
+    for group in [two, four, one, three] + share:
+        for j in chunks:
+            group[j].wait_send()
+
+
+def gather_window(conv_out):
+    count = lax.axis_size("seq")
+    rows, width = conv_out.shape
+    slots = 2 * REACH_CHIPS + 2
+    return pl.pallas_call(
+        functools.partial(window_kernel, count),
+        out_shape=jax.ShapeDtypeStruct((slots * rows, width), conv_out.dtype),
+        in_specs=[pl.BlockSpec(memory_space=pltpu.VMEM)],
+        out_specs=pl.BlockSpec(memory_space=pltpu.VMEM),
+        scratch_shapes=[
+            pltpu.SemaphoreType.DMA((9, CHUNKS)),
+            pltpu.SemaphoreType.DMA((9, CHUNKS)),
+        ],
+        compiler_params=pltpu.CompilerParams(
+            collective_id=1, has_side_effects=True, vmem_limit_bytes=48 * 1024 * 1024
+        ),
+        cost_estimate=pl.CostEstimate(
+            flops=0, bytes_accessed=2 * slots * rows * width, transcendentals=0
+        ),
+        name="gather_window",
+    )(conv_out)
+
+
+def attention_kernel(tok_rows, q_ref, k_ref, v_ref, out_w_ref, gain_ref, o_ref, att_ref):
     pair = pl.program_id(0)
     pairs = pl.num_programs(0)
     rank = lax.axis_index("seq")
-    past = kp_ref.shape[0]
+    past = 2 * REACH_CHIPS * tok_rows
+    shift = pl.multiple_of(lax.rem(rank, 2) * tok_rows, tok_rows)
+    old = pl.ds(shift, tok_rows)
+    mid = pl.ds(pl.multiple_of(shift + tok_rows, tok_rows), past - tok_rows)
+    new = pl.ds(pl.multiple_of(shift + past, tok_rows), tok_rows)
     lanes = q_ref.shape[1]
     low_half = lax.broadcasted_iota(jnp.int32, (tok_rows, lanes), 1) < HEAD
     row = lax.broadcasted_iota(jnp.int32, (tok_rows, tok_rows), 0)
@@ -99,9 +196,9 @@
     for half in range(2):
         keep = low_half if half == 0 else jnp.logical_not(low_half)
         q_head = jnp.where(keep, scaled, jnp.zeros_like(scaled))
-        s_mid = lax.dot_general(q_head, kp_ref[tok_rows:, :], nt, preferred_element_type=jnp.float32)
-        s_old = lax.dot_general(q_head, kp_ref[:tok_rows, :], nt, preferred_element_type=jnp.float32)
-        s_new = lax.dot_general(q_head, kl_ref[...], nt, preferred_element_type=jnp.float32)
+        s_mid = lax.dot_general(q_head, k_ref[mid, :], nt, preferred_element_type=jnp.float32)
+        s_old = lax.dot_general(q_head, k_ref[old, :], nt, preferred_element_type=jnp.float32)
+        s_new = lax.dot_general(q_head, k_ref[new, :], nt, preferred_element_type=jnp.float32)
         s_mid = jnp.where(mid_col >= absent, s_mid, -jnp.inf)
         s_old = jnp.where(col >= absent, s_old, -jnp.inf)
         s_edge = jnp.where(recent, s_new, s_old)
@@ -117,9 +214,9 @@
         p_new = jnp.where(recent, p_edge, 0.0).astype(jnp.bfloat16)
         p_old = jnp.where(recent, 0.0, p_edge).astype(jnp.bfloat16)
         halves.append(
-            jnp.dot(p_mid, vp_ref[tok_rows:, :], preferred_element_type=jnp.float32)
-            + jnp.dot(p_old, vp_ref[:tok_rows, :], preferred_element_type=jnp.float32)
-            + jnp.dot(p_new, vl_ref[...], preferred_element_type=jnp.float32)
+            jnp.dot(p_mid, v_ref[mid, :], preferred_element_type=jnp.float32)
+            + jnp.dot(p_old, v_ref[old, :], preferred_element_type=jnp.float32)
+            + jnp.dot(p_new, v_ref[new, :], preferred_element_type=jnp.float32)
         )
     att_ref[:, pl.ds(pl.multiple_of(pair * lanes, lanes), lanes)] = jnp.where(
         low_half, halves[0], halves[1]
@@ -134,20 +231,19 @@
         ).astype(o_ref.dtype)
 
 
-def attention(qkv, past_kv, out_weight, gain, tok_rows, model_width):
+def attention(query, key_value, out_weight, gain, tok_rows, model_width):
     lanes = 2 * HEAD
     pairs = model_width // lanes
-    past = past_kv.shape[0]
+    span = key_value.shape[0]
+    past = 2 * REACH_CHIPS * tok_rows
     return pl.pallas_call(
         functools.partial(attention_kernel, tok_rows),
         grid=(pairs,),
         out_shape=jax.ShapeDtypeStruct((tok_rows, model_width), jnp.bfloat16),
         in_specs=[
             pl.BlockSpec((tok_rows, lanes), lambda h: (0, h)),
-            pl.BlockSpec((past, lanes), lambda h: (0, h)),
-            pl.BlockSpec((past, lanes), lambda h: (0, pairs + h)),
-            pl.BlockSpec((tok_rows, lanes), lambda h: (0, pairs + h)),
-            pl.BlockSpec((tok_rows, lanes), lambda h: (0, 2 * pairs + h)),
+            pl.BlockSpec((span, lanes), lambda h: (0, h)),
+            pl.BlockSpec((span, lanes), lambda h: (0, pairs + h)),
             pl.BlockSpec(out_weight.shape, lambda h: (0, 0)),
             pl.BlockSpec(gain.shape, lambda h: (0, 0)),
         ],
@@ -160,7 +256,7 @@
             transcendentals=tok_rows * past * model_width // HEAD,
         ),
         name="window_attention",
-    )(qkv, past_kv, past_kv, qkv, qkv, out_weight, gain)
+    )(query, key_value, key_value, out_weight, gain)
 
 
 def solution(mesh):

time: 245 us -> 159 us (0.65)
  the two profiles are of different devices: /device:TPU:18 before, /device:TPU:0 now
where the time goes in v2:
time: 159 us; the launch traced here: 158 us
  Pallas kernels  60.1 us (38%)
  waiting for transfers between devices  27.9 us (18%)
  matrix products  19.2 us (12%)
  local copies, waits for them, and re-layouts  13.6 us (9%)
  blocking collectives  13.6 us (9%)
  between operations  13.5 us (8%)
  starting transfers between devices  6.5 us (4%)
  other arithmetic  4.19 us (3%)
    pallas_call x1, Pallas kernels, gather_window(): pl.pallas_call(functools.partial(window_kernel, count), out_shape=jax.Sha...  36.7 us
    pallas_call x1, Pallas kernels, attention(): pl.pallas_call(functools.partial(attention_kernel, tok_rows), grid=(pairs...  23.3 us
    all_to_all x1, waiting for transfers between devices, local(): lax.all_to_all(found, 'seq', split_axis=0, concat_axis=0, tiled=True)  22.1 us
    dot_general x1, matrix products, local(): jnp.dot(window, full_qkv[:, model_width:], preferred_element_type=jnp.flo...  16.9 us
    all_to_all x1, blocking collectives, local(): lax.all_to_all(request_table, 'seq', split_axis=0, concat_axis=0, tiled=T...  13.6 us
    gather x1, local copies, waits for them, and re-layouts, local(): variant_table[lax.all_to_all(request_table, 'seq', split_axis=0, concat_a...  6.57 us
    unnamed x12, local copies, waits for them, and re-layouts  3.91 us
    all_to_all x1, starting transfers between devices, local(): lax.all_to_all(found, 'seq', split_axis=0, concat_axis=0, tiled=True)  3.79 us
  transfers between devices with their start and end apart: 4, of which 3 were waited for; matrix products, arithmetic and copies ran while one was open for 21% of the time, Pallas kernels for 23%

profile of v2, /device:TPU:0, one launch (start us, length us, event | category | flops | bytes accessed | tf_op | source)
XLA Modules:
  0.0 158.5 jit_solution(11984790871512019267)
XLA Ops:
  6.5 0.7 all-gather.3.cloned.1.call-update
  7.3 0.7 fusion.14
  7.9 0.6 reduce-window.6
  8.5 0.2 slice_reduce_fusion
  8.7 0.8 fusion.13
  9.5 0.7 compare_select_fusion.1
  10.2 1.6 scatter_custom_fusion
  11.8 0.1 all_to_all.11
  11.8 13.6 %all_to_all.17 = s32[16,1,32]{2,1,0:T(1,128)S(1)} all-to-all(s32[16,1,32]{2,1,0:T(1,128)S(1)} %all_to_all.11), channel_id=1, replica_groups=mesh['seq'=16,'fsdp'=2] {'seq'}, dimensions={0} | all-to-all | bytes 4096 | tf_op jit(solution)/shard_map/all_to_all | solution.py:54
  25.4 0.1 reshape.103
  25.5 6.6 %gather_fusion = bf16[512,1024]{1,0:T(8,128)(2,1)} fusion(bf16[2048,1024]{1,0:T(8,128)(2,1)} %param.12, s32[1024]{0:T(1024)S(1)} %pad_clamp_fusion.1), kind=kCustom, calls=%fused_computation | custom fusion | bytes 2099200 | tf_op jit(solution)/shard_map/gather | solution.py:53
  32.1 3.8 %all-to-all-start.1 = ((bf16[16,32,1024]{2,1,0:T(8,128)(2,1)}), bf16[16,32,1024]{2,1,0:T(8,128)(2,1)S(1)}, u32[]{:S(2)}, u32[]{:S(2)}) async-start(bf16[16,32,1024]{2,1,0:T(8,128)(2,1)} %bitcast.10), calls=%async_computation.1 | async-start | bytes 2097152 | tf_op jit(solution)/shard_map/all_to_all | solution.py:56
  35.9 0.0 all-gather.5.cloned.1.call-start
  36.0 0.7 all-gather.5.cloned.1.call-update
  36.7 22.1 %all-to-all-done.1 = bf16[16,32,1024]{2,1,0:T(8,128)(2,1)S(1)} async-done(((bf16[16,32,1024]{2,1,0:T(8,128)(2,1)}), bf16[16,32,1024]{2,1,0:T(8,128)(2,1)S(1)}, u32[]{:S(2)}, u32[]{:S(2)}) %all-to-all-start.1) | async-done | bytes 1048608 | tf_op jit(solution)/shard_map/all_to_all | solution.py:56
  58.8 1.2 gather_fusion.1
  60.0 0.3 multiply_reduce_fusion
  60.2 0.2 multiply_convert_fusion
  60.5 2.7 %collective-permute-start = (bf16[6,1024]{1,0:T(8,128)(2,1)S(1)}, bf16[6,1024]{1,0:T(8,128)(2,1)S(1)}, u32[]{:S(2)}, u32[]{:S(2)}) collective-permute-start(bf16[6,1024]{1,0:T(8,128)(2,1)S(1)} %slice.77), channel_id=1, source_target_pairs={{0,2},{2,4},{4,6},{6,8},{8,10},{10,12},{12,14},{14,16},{16,18},{18... | collective-permute-start | bytes 36872 | tf_op jit(solution)/shard_map/ppermute | solution.py:20
  63.2 0.0 copy-done.4
  63.2 0.6 collective-permute-done
  63.8 0.9 add_convert_fusion.conv_ref
  64.7 36.7 %gather_window.1 = bf16[2560,1024]{1,0:T(8,128)(2,1)S(1)} custom-call(bf16[256,1024]{1,0:T(8,128)(2,1)S(1)} %add_convert_fusion.conv_ref), custom_call_target="tpu_custom_call" | custom-call | bytes 5242880 | tf_op jit(solution)/shard_map/gather_window/pallas_call | solution.py:157
  101.5 0.0 copy-start
  101.5 2.3 %copy-done = bf16[2560,1024]{1,0:T(8,128)(2,1)} copy-done((bf16[2560,1024]{1,0:T(8,128)(2,1)}, bf16[2560,1024]{1,0:T(8,128)(2,1)S(1)}, u32[]{:S(2)}) %copy-start) | copy-done | bytes 5242904
  103.8 2.3 %fusion.3.q_ref = bf16[256,1024]{1,0:T(8,128)(2,1)S(1)} fusion(bf16[256,1024]{1,0:T(8,128)(2,1)S(1)} %add_convert_fusion.conv_ref, bf16[1024,3072]{1,0:T(8,128)(2,1)} %all-gather.3.cloned.1.call-done), kind=kOutput, calls=%fused_computation.12 | convolution fusion | flops 537133056 | bytes 3145728 | tf_op jit(solution)/shard_map/dot_general | solution.py:74
  106.1 0.0 copy-start.2
  106.1 16.9 %convolution_convert_fusion.k_ref.v_ref = bf16[2560,2048]{1,0:T(8,128)(2,1)} fusion(bf16[2560,1024]{1,0:T(8,128)(2,1)} %copy-done, bf16[1024,3072]{1,0:T(8,128)(2,1)} %all-gather.3.cloned.1.call-done), kind=kOutput, calls=%fused_computation.3 | convolution fusion | flops 10742661120 | bytes 19922944 | tf_op jit(solution)/shard_map/dot_general | solution.py:77
  123.0 3.7 %all-gather.5.cloned.1.call-done.out_w_ref = bf16[1024,1024]{1,0:T(8,128)(2,1)} async-done(((bf16[1024,512]{1,0:T(8,128)(2,1)}), bf16[1024,1024]{1,0:T(8,128)(2,1)}) %all-gather.5.cloned.1.call-update) | async-done | bytes 2097168 | tf_op jit(solution)/shard_map/all_gather | solution.py:71
  126.7 0.0 copy-done.2
  126.7 1.6 %copy-done.1 = bf16[1024,1024]{1,0:T(8,128)(2,1)S(1)} copy-done((bf16[1024,1024]{1,0:T(8,128)(2,1)S(1)}, bf16[1024,1024]{1,0:T(8,128)(2,1)}, u32[]{:S(2)}) %copy-start.1) | copy-done | bytes 2097176
  128.3 23.3 %window_attention.1 = bf16[256,1024]{1,0:T(8,128)(2,1)} custom-call(bf16[256,1024]{1,0:T(8,128)(2,1)S(1)} %fusion.3.q_ref, bf16[2560,2048]{1,0:T(8,128)(2,1)} %convolution_convert_fusion.k_ref.v_ref, bf16[2560,2048]{1,0:T(8,128)(2,1)} %convolution_convert_fusion.k_ref.v_ref, bf16[1024,1024]{1,0:T(8,128)(2,1)S(1)} %copy-done.1, f32[1,1024]{1,0:T(1,128)S(1)} %bitcast.48), custom_call_target="tpu_custom_call" | custom-call | flops 4831838208 | bytes 8388608 | tf_op jit(solution)/shard_map/window_attention/pallas_call | solution.py:239
  (16 shorter events, 0.1 us)
Async XLA Ops:
  6.5 97.2 %all-gather.3.cloned.1.call-start = ((), (), s32[]{:S(2)}) async-start(), calls=%async_computation.2 | async-start | bytes 9437184 | tf_op jit(solution)/shard_map/all_gather | solution.py:70
  32.1 27.9 %copy-start.3 = (bf16[1,256,1024]{2,1,0:T(8,128)(2,1)S(1)}, bf16[1,256,1024]{2,1,0:T(8,128)(2,1)}, u32[]{:S(2)}) copy-start(bf16[1,256,1024]{2,1,0:T(8,128)(2,1)} %param.9) | copy-start | bytes 1572868
  32.1 28.1 %copy-start.5 = (f32[1024]{0:T(1024)S(1)}, f32[1024]{0:T(1024)}, u32[]{:S(2)}) copy-start(f32[1024]{0:T(1024)} %param.13) | copy-start | bytes 12292
  32.1 31.1 %copy-start.4 = (bf16[7,1024]{1,0:T(8,128)(2,1)S(1)}, bf16[7,1024]{1,0:T(8,128)(2,1)}, u32[]{:S(2)}) copy-start(bf16[7,1024]{1,0:T(8,128)(2,1)} %param.14) | copy-start | bytes 43012
  32.1 26.7 %all-to-all-start.1 = ((bf16[16,32,1024]{2,1,0:T(8,128)(2,1)}), bf16[16,32,1024]{2,1,0:T(8,128)(2,1)S(1)}, u32[]{:S(2)}, u32[]{:S(2)}) async-start(bf16[16,32,1024]{2,1,0:T(8,128)(2,1)} %bitcast.10), calls=%async_computation.1 | async-start | bytes 2097152 | tf_op jit(solution)/shard_map/all_to_all | solution.py:56
  35.9 90.8 %all-gather.5.cloned.1.call-start = ((), (), s32[]{:S(2)}) async-start(), calls=%async_computation.3 | async-start | bytes 3145728 | tf_op jit(solution)/shard_map/all_gather | solution.py:71
  60.5 3.3 %collective-permute-start = (bf16[6,1024]{1,0:T(8,128)(2,1)S(1)}, bf16[6,1024]{1,0:T(8,128)(2,1)S(1)}, u32[]{:S(2)}, u32[]{:S(2)}) collective-permute-start(bf16[6,1024]{1,0:T(8,128)(2,1)S(1)} %slice.77), channel_id=1, source_target_pairs={{0,2},{2,4},{4,6},{6,8},{8,10},{10,12},{12,14},{14,16},{16,18},{18... | collective-permute-start | bytes 36872 | tf_op jit(solution)/shard_map/ppermute | solution.py:20
  101.5 2.3 %copy-start = (bf16[2560,1024]{1,0:T(8,128)(2,1)}, bf16[2560,1024]{1,0:T(8,128)(2,1)S(1)}, u32[]{:S(2)}) copy-start(bf16[2560,1024]{1,0:T(8,128)(2,1)S(1)} %gather_window.1) | copy-start | bytes 15728644
  106.1 20.6 %copy-start.2 = (f32[1024]{0:T(1024)S(1)}, f32[1024]{0:T(1024)}, u32[]{:S(2)}) copy-start(f32[1024]{0:T(1024)} %param.17) | copy-start | bytes 12292
  126.7 1.6 %copy-start.1 = (bf16[1024,1024]{1,0:T(8,128)(2,1)S(1)}, bf16[1024,1024]{1,0:T(8,128)(2,1)}, u32[]{:S(2)}) copy-start(bf16[1024,1024]{1,0:T(8,128)(2,1)} %all-gather.5.cloned.1.call-done.out_w_ref) | copy-start | bytes 6291460
Sparse Core Ops, SparseCore 0:
  8.9 83.0 all-gather.2
  93.5 33.1 all-gather.4

commit v3 on v2

--- a/solution.py
+++ b/solution.py
@@ -12,12 +12,6 @@
 
 
 EPSILON = 1e-05
-
-
-def shifted(value, axis, steps):
-    count = lax.axis_size(axis)
-    first, last = (max(0, -steps), min(count, count - steps))
-    return lax.ppermute(value, axis, [(source, source + steps) for source in range(first, last)])
 
 
 def rms_scale(values, gain):
@@ -35,11 +29,10 @@
     out_weight,
     attn_gain,
 ):
-    seq_rank = lax.axis_index("seq")
     seq_count = lax.axis_size("seq")
     tok_rows = dna_embed.shape[1]
     model_width = dna_embed.shape[2]
-    slot_count = max(2, 2 * tok_rows // seq_count)
+    slot_count = max(16, 2 * tok_rows // seq_count)
     owner_ids = site_owner[0, :, 0]
     wanted_rows = site_row[0]
     owner_onehot = (owner_ids[:, None] == jnp.arange(seq_count, dtype=jnp.int32)[None, :]).astype(
@@ -49,28 +42,17 @@
     rank_within = jnp.sum(earlier_same * owner_onehot, axis=1)
     slot_index = owner_ids * slot_count + rank_within
     request_table = jnp.zeros((seq_count * slot_count,), jnp.int32).at[slot_index].set(wanted_rows)
-    request_table = request_table.reshape(seq_count, slot_count)
-    found = variant_table[
-        lax.all_to_all(request_table, "seq", split_axis=0, concat_axis=0, tiled=True)
-    ]
-    fetched = lax.all_to_all(found, "seq", split_axis=0, concat_axis=0, tiled=True)
-    site_embed = fetched.reshape(seq_count * slot_count, model_width)[slot_index]
-    resid = dna_embed[0].astype(jnp.float32) + site_embed.astype(jnp.float32)
-    normed = rms_scale(resid, norm_gain).astype(jnp.bfloat16)
-    taps = conv_weight.shape[0]
-    rim_rows = shifted(normed[tok_rows - (taps - 1) :], "seq", 1)
-    padded = jnp.concatenate([rim_rows, normed], axis=0)
-    conv_sum = jnp.zeros((tok_rows, model_width), jnp.float32)
-    for tap in range(taps):
-        conv_sum = conv_sum + conv_weight[tap].astype(jnp.float32) * padded[
-            taps - 1 - tap : taps - 1 - tap + tok_rows
-        ].astype(jnp.float32)
-    conv_out = conv_sum.astype(jnp.bfloat16)
-    full_qkv, full_out = (
-        lax.all_gather(qkv_weight, "fsdp", axis=1, tiled=True),
-        lax.all_gather(out_weight, "fsdp", axis=1, tiled=True),
-    )
-    window = gather_window(conv_out)
+    conv_out, full_qkv = embed_and_conv(
+        jnp.broadcast_to(request_table[:, None], (seq_count * slot_count, LANES)),
+        slot_index[:, None],
+        dna_embed[0],
+        variant_table,
+        norm_gain[None, :],
+        conv_weight,
+        qkv_weight,
+        slot_count,
+    )
+    window, full_out = gather_window(conv_out, out_weight)
     query = jnp.dot(
         conv_out, full_qkv[:, :model_width], preferred_element_type=jnp.float32
     ).astype(jnp.bfloat16)
@@ -85,7 +67,9 @@
 REACH_CHIPS = 4
 
 
-def window_kernel(count, conv_ref, win_ref, send_sem, recv_sem):
+def window_kernel(
+    count, conv_ref, shard_ref, win_ref, full_ref, send_sem, recv_sem, swap_sem, local_sem
+):
     me = lax.axis_index("seq")
     rows = conv_ref.shape[0]
     part = rows // CHUNKS
@@ -106,7 +90,12 @@
     barrier = pltpu.get_barrier_semaphore()
     for other in (ahead, behind, beside, twin):
         pl.semaphore_signal(barrier, inc=1, device_id={"seq": other}, device_id_type=MESH)
-    pl.semaphore_wait(barrier, 4)
+    pl.semaphore_signal(
+        barrier, inc=1, device_id={"fsdp": 1 - lax.axis_index("fsdp")}, device_id_type=MESH
+    )
+    pl.semaphore_wait(barrier, 5)
+    swap = WeightSwap(shard_ref, full_ref, swap_sem, local_sem, 1)
+    swap.start()
 
     def message(kind, chunk, source_back, target_back, target):
         return pltpu.make_async_remote_copy(
@@ -148,20 +137,26 @@
     for group in [two, four, one, three] + share:
         for j in chunks:
             group[j].wait_send()
-
-
-def gather_window(conv_out):
+    swap.finish()
+
+
+def gather_window(conv_out, shard):
     count = lax.axis_size("seq")
     rows, width = conv_out.shape
     slots = 2 * REACH_CHIPS + 2
     return pl.pallas_call(
         functools.partial(window_kernel, count),
-        out_shape=jax.ShapeDtypeStruct((slots * rows, width), conv_out.dtype),
-        in_specs=[pl.BlockSpec(memory_space=pltpu.VMEM)],
-        out_specs=pl.BlockSpec(memory_space=pltpu.VMEM),
+        out_shape=[
+            jax.ShapeDtypeStruct((slots * rows, width), conv_out.dtype),
+            jax.ShapeDtypeStruct((shard.shape[0], 2 * shard.shape[1]), shard.dtype),
+        ],
+        in_specs=[pl.BlockSpec(memory_space=pltpu.VMEM), pl.BlockSpec(memory_space=pl.ANY)],
+        out_specs=[pl.BlockSpec(memory_space=pltpu.VMEM), pl.BlockSpec(memory_space=pl.ANY)],
         scratch_shapes=[
             pltpu.SemaphoreType.DMA((9, CHUNKS)),
             pltpu.SemaphoreType.DMA((9, CHUNKS)),
+            pltpu.SemaphoreType.DMA((4, 1)),
+            pltpu.SemaphoreType.DMA,
         ],
         compiler_params=pltpu.CompilerParams(
             collective_id=1, has_side_effects=True, vmem_limit_bytes=48 * 1024 * 1024
@@ -170,7 +165,213 @@
             flops=0, bytes_accessed=2 * slots * rows * width, transcendentals=0
         ),
         name="gather_window",
-    )(conv_out)
+    )(conv_out, shard)
+
+
+LANES = 128
+EDGE = 16
+
+
+class WeightSwap:
+    def __init__(self, shard_ref, full_ref, sems, local_sem, parts):
+        me = lax.axis_index("seq")
+        half = lax.axis_index("fsdp")
+        core = lax.rem(me, 2)
+        rows, cols = shard_ref.shape
+        part = rows // 2 // parts
+
+        def block(ref, chunk, column):
+            first = pl.multiple_of(core * (rows // 2) + chunk * part, part)
+            return ref.at[pl.ds(first, part), pl.ds(pl.multiple_of(column * cols, LANES), cols)]
+
+        self.own = pltpu.make_async_copy(
+            shard_ref, full_ref.at[:, pl.ds(pl.multiple_of(half * cols, LANES), cols)], local_sem
+        )
+        self.across = [
+            pltpu.make_async_remote_copy(
+                src_ref=block(shard_ref, j, 0),
+                dst_ref=block(full_ref, j, half),
+                send_sem=sems.at[0, j],
+                recv_sem=sems.at[1, j],
+                device_id={"fsdp": 1 - half},
+                device_id_type=MESH,
+            )
+            for j in range(parts)
+        ]
+        self.pass_on = [
+            pltpu.make_async_remote_copy(
+                src_ref=block(full_ref, j, 1 - half),
+                dst_ref=block(full_ref, j, 1 - half),
+                send_sem=sems.at[2, j],
+                recv_sem=sems.at[3, j],
+                device_id={"seq": me + 1 - 2 * core},
+                device_id_type=MESH,
+            )
+            for j in range(parts)
+        ]
+
+    def start(self):
+        for copy in self.across:
+            copy.start()
+        self.own.start()
+
+    def finish(self):
+        for arrive, give in zip(self.across, self.pass_on):
+            arrive.wait_recv()
+            give.start()
+        self.own.wait()
+        for arrive, give in zip(self.across, self.pass_on):
+            arrive.wait_send()
+            give.wait()
+
+
+def embed_kernel(
+    count, slots, request_ref, slot_ref, dna_ref, table_ref, gain_ref, taps_ref, shard_ref,
+    conv_ref, full_ref,
+    inbox, found, fetched, edge_out, edge_in,
+    ask_send, ask_recv, give_send, give_recv, edge_sem, swap_sem, local_sem,
+):
+    me = lax.axis_index("seq")
+    rows = dna_ref.shape[0]
+    site_rows = table_ref.shape[0]
+    batch = LANES // slots
+
+    def at(ref, index):
+        return ref.at[pl.ds(pl.multiple_of(index * slots, slots), slots)]
+
+    def ask(step):
+        target = lax.rem(me + step, count)
+        return pltpu.make_async_remote_copy(
+            src_ref=at(request_ref, target),
+            dst_ref=at(inbox, step),
+            send_sem=ask_send.at[step],
+            recv_sem=ask_recv.at[step],
+            device_id={"seq": target},
+            device_id_type=MESH,
+        )
+
+    def give(step):
+        return pltpu.make_async_remote_copy(
+            src_ref=at(found, step),
+            dst_ref=at(fetched, me),
+            send_sem=give_send.at[step],
+            recv_sem=give_recv.at[step],
+            device_id={"seq": lax.rem(me + count - step, count)},
+            device_id_type=MESH,
+        )
+
+    swap = WeightSwap(shard_ref, full_ref, swap_sem, local_sem, 2)
+    barrier = pltpu.get_barrier_semaphore()
+
+    def greet(step, carry):
+        pl.semaphore_signal(
+            barrier, inc=1, device_id={"seq": lax.rem(me + step, count)}, device_id_type=MESH
+        )
+        return carry
+
+    lax.fori_loop(1, count, greet, 0)
+    pl.semaphore_signal(
+        barrier, inc=1, device_id={"fsdp": 1 - lax.axis_index("fsdp")}, device_id_type=MESH
+    )
+    pl.semaphore_wait(barrier, count)
+
+    def each(first, action):
+        def body(step, carry):
+            action(step)
+            return carry
+
+        lax.fori_loop(first, count, body, 0)
+
+    each(1, lambda step: ask(step).start())
+    swap.start()
+    inbox[0:slots, :] = request_ref[pl.ds(pl.multiple_of(me * slots, slots), slots), :]
+    lane = lax.broadcasted_iota(jnp.int32, (LANES, LANES), 1)
+    for group in range(count // batch):
+        steps = range(group * batch, (group + 1) * batch)
+        for step in steps:
+            if step > 0:
+                ask(step).wait_recv()
+        ids = inbox[group * LANES : (group + 1) * LANES, :]
+        pick = jnp.concatenate(
+            [
+                jnp.where(ids - base == lane, 1.0, 0.0).astype(jnp.bfloat16)
+                for base in range(0, site_rows, LANES)
+            ],
+            axis=1,
+        )
+        got = jnp.dot(pick, table_ref[...], preferred_element_type=jnp.float32)
+        found[group * LANES : (group + 1) * LANES, :] = got.astype(jnp.bfloat16)
+        for step in steps:
+            if step > 0:
+                give(step).start()
+    fetched[pl.ds(pl.multiple_of(me * slots, slots), slots), :] = found[0:slots, :]
+    each(1, lambda step: give(step).wait_recv())
+
+    place = lax.broadcasted_iota(jnp.int32, (rows, count * slots), 1)
+    pick = jnp.where(slot_ref[...] == place, 1.0, 0.0).astype(jnp.bfloat16)
+    site_embed = jnp.dot(pick, fetched[...], preferred_element_type=jnp.float32)
+    resid = dna_ref[...].astype(jnp.float32) + site_embed
+    normed = rms_scale(resid, gain_ref[...]).astype(jnp.bfloat16)
+    edge_out[...] = normed[rows - EDGE :, :]
+    edge = pltpu.make_async_remote_copy(
+        src_ref=edge_out,
+        dst_ref=edge_in,
+        send_sem=edge_sem.at[0],
+        recv_sem=edge_sem.at[1],
+        device_id={"seq": lax.rem(me + 1, count)},
+        device_id_type=MESH,
+    )
+    edge.start()
+    edge.wait()
+    before = jnp.where(me > 0, edge_in[...].astype(jnp.float32), 0.0)
+    padded = jnp.concatenate([before, normed.astype(jnp.float32)], axis=0)
+    total = jnp.zeros(dna_ref.shape, jnp.float32)
+    for tap in range(taps_ref.shape[0]):
+        total = total + taps_ref[tap : tap + 1, :].astype(jnp.float32) * padded[
+            EDGE - tap : EDGE - tap + rows
+        ]
+    conv_ref[...] = total.astype(jnp.bfloat16)
+    each(1, lambda step: ask(step).wait_send())
+    each(1, lambda step: give(step).wait_send())
+    swap.finish()
+
+
+def embed_and_conv(requests, slot_index, dna, table, gain, taps, shard, slots):
+    count = lax.axis_size("seq")
+    rows, width = dna.shape
+    vmem = pl.BlockSpec(memory_space=pltpu.VMEM)
+    anywhere = pl.BlockSpec(memory_space=pl.ANY)
+    dma = pltpu.SemaphoreType.DMA
+    return pl.pallas_call(
+        functools.partial(embed_kernel, count, slots),
+        out_shape=[
+            jax.ShapeDtypeStruct((rows, width), jnp.bfloat16),
+            jax.ShapeDtypeStruct((shard.shape[0], 2 * shard.shape[1]), shard.dtype),
+        ],
+        in_specs=[vmem] * 6 + [anywhere],
+        out_specs=[vmem, anywhere],
+        scratch_shapes=[
+            pltpu.VMEM((count * slots, LANES), jnp.int32),
+            pltpu.VMEM((count * slots, width), jnp.bfloat16),
+            pltpu.VMEM((count * slots, width), jnp.bfloat16),
+            pltpu.VMEM((EDGE, width), jnp.bfloat16),
+            pltpu.VMEM((EDGE, width), jnp.bfloat16),
+            dma((count,)),
+            dma((count,)),
+            dma((count,)),
+            dma((count,)),
+            dma((2,)),
+            dma((4, 2)),
+            dma,
+        ],
+        compiler_params=pltpu.CompilerParams(
+            collective_id=2, has_side_effects=True, vmem_limit_bytes=48 * 1024 * 1024
+        ),
+        cost_estimate=pl.CostEstimate(
+            flops=4 * rows * table.size, bytes_accessed=2 * table.size, transcendentals=0
+        ),
+        name="embed_and_conv",
+    )(requests, slot_index, dna, table, gain, taps, shard)
 
 
 def attention_kernel(tok_rows, q_ref, k_ref, v_ref, out_w_ref, gain_ref, o_ref, att_ref):

time: 159 us -> 140 us (0.88)
  Pallas kernels: 60.1 us -> 111 us
  waiting for transfers between devices: 27.9 us -> 0 us
  blocking collectives: 13.6 us -> 0 us
  between operations: 13.5 us -> 0.09 us
  local copies, waits for them, and re-layouts: 13.6 us -> 6.48 us
  starting transfers between devices: 6.5 us -> 0 us
    pallas_call x1 -> x2, Pallas kernels: 36.7 us -> 87.3 us  [the longest x1 49.3 us: embed_and_conv(): pl.pallas_call(functools.partial(embed_kernel, count, slots), out_shape=[...]
    all_to_all x1 -> x0, waiting for transfers between devices: 22.1 us -> none  [local(): lax.all_to_all(found, 'seq', split_axis=0, concat_axis=0, tiled=True)]
    all_to_all x1 -> x0, blocking collectives: 13.6 us -> none  [local(): lax.all_to_all(request_table, 'seq', split_axis=0, concat_axis=0, tiled=T...]
    gather x2 -> x0, local copies, waits for them, and re-layouts: 7.74 us -> none  [the longest x1 6.57 us: local(): variant_table[lax.all_to_all(request_table, 'seq', split_axis=0, concat_a...]
    all_to_all x1 -> x0, starting transfers between devices: 3.79 us -> none  [local(): lax.all_to_all(found, 'seq', split_axis=0, concat_axis=0, tiled=True)]
    all_gather x2 -> x0, waiting for transfers between devices: 3.74 us -> none  [the longest x1 3.74 us: local(): lax.all_gather(out_weight, 'fsdp', axis=1, tiled=True)]
    ppermute x1 -> x0, starting transfers between devices: 2.67 us -> none  [shifted(): lax.ppermute(value, axis, [(source, source + steps) for source in range(f...]
  transfers between devices with their start and end apart: 4 -> 0, of which waited for: 3 -> 0; matrix products, arithmetic and copies ran while one was open for 21% -> 0% of each run, Pallas kernels for 23% -> 0%
where the time goes in v3:
time: 140 us; the launch traced here: 139 us
  Pallas kernels  111 us (79%)
  matrix products  19.2 us (14%)
  local copies, waits for them, and re-layouts  6.48 us (5%)
  other arithmetic  2.87 us (2%)
    pallas_call x1, Pallas kernels, embed_and_conv(): pl.pallas_call(functools.partial(embed_kernel, count, slots), out_shape=[...  49.3 us
    pallas_call x1, Pallas kernels, gather_window(): pl.pallas_call(functools.partial(window_kernel, count), out_shape=[jax.Sh...  37.9 us
    pallas_call x1, Pallas kernels, attention(): pl.pallas_call(functools.partial(attention_kernel, tok_rows), grid=(pairs...  23.4 us
    dot_general x1, matrix products, local(): jnp.dot(window, full_qkv[:, model_width:], preferred_element_type=jnp.flo...  16.9 us
    unnamed x12, local copies, waits for them, and re-layouts  4.34 us

profile of v3, /device:TPU:0, one launch (start us, length us, event | category | flops | bytes accessed | tf_op | source)
XLA Modules:
  0.0 139.3 jit_solution(10030067667727119161)
XLA Ops:
  0.0 0.7 multiply_bitcast_fusion
  0.7 0.7 fusion.10
  1.4 0.6 reduce-window.6
  1.9 0.2 slice_reduce_fusion
  2.2 0.8 fusion.9
  2.9 0.1 copy.12
  3.1 0.1 copy.11
  3.2 0.1 fusion.6
  3.3 1.6 %scatter_custom_fusion = s32[512]{0:T(512)S(1)} fusion(s32[256]{0:T(256)S(1)} %get-tuple-element.13, s32[256]{0:T(256)} %bitcast.38, s32[]{:T(128)} %constant.3.clone.1), kind=kCustom, calls=%fused_computation.18 | custom fusion | bytes 2560 | tf_op jit(solution)/shard_map/scatter | solution.py:44
  4.9 0.1 broadcast_in_dim.22.request_ref
  5.0 0.0 copy-start
  5.1 1.9 %copy-done = bf16[1024,1536]{1,0:T(8,128)(2,1)S(1)} copy-done((bf16[1024,1536]{1,0:T(8,128)(2,1)S(1)}, bf16[1024,1536]{1,0:T(8,128)(2,1)}, u32[]{:S(2)}) %copy-start) | copy-done | bytes 3145752
  6.9 0.0 copy-start.2
  6.9 1.0 copy-done.2
  8.0 0.0 copy-start.3
  8.0 0.7 copy-done.3
  8.7 0.0 copy-start.4
  8.7 0.7 copy-done.4
  9.4 0.0 copy-start.1
  9.4 49.3 %embed_and_conv.1 = (bf16[256,1024]{1,0:T(8,128)(2,1)S(1)}, bf16[1024,3072]{1,0:T(8,128)(2,1)}) custom-call(s32[512,128]{1,0:T(8,128)S(1)} %broadcast_in_dim.22.request_ref, s32[256,1]{1,0:T(8,128)S(1)} %get-tuple-element.14.slot_ref, bf16[256,1024]{1,0:T(8,128)(2,1)S(1)} %bitcast.32, bf16[2048,1024]{1,0:T(8,128)(2,1)} %table_ref.1, f32[1,1024]{1,0:T(1,128)S(1)} %bitcast.33, ...), custom_call_target="tpu_custom_call" | custom-call | flops 2147483648 | bytes 4194304 | tf_op jit(solution)/shard_map/embed_and_conv/pallas_call | solution.py:345
  58.7 2.3 %fusion.3.q_ref = bf16[256,1024]{1,0:T(8,128)(2,1)S(1)} fusion(bf16[256,1024]{1,0:T(8,128)(2,1)S(1)} %get-tuple-element.9.conv_ref, bf16[1024,3072]{1,0:T(8,128)(2,1)} %get-tuple-element.10), kind=kOutput, calls=%fused_computation.5 | convolution fusion | flops 537133056 | bytes 3145728 | tf_op jit(solution)/shard_map/dot_general | solution.py:56
  61.1 0.0 copy-done.1
  61.1 37.9 %gather_window.1 = (bf16[2560,1024]{1,0:T(8,128)(2,1)}, bf16[1024,1024]{1,0:T(8,128)(2,1)S(1)}) custom-call(bf16[256,1024]{1,0:T(8,128)(2,1)S(1)} %get-tuple-element.9.conv_ref, bf16[1024,512]{1,0:T(8,128)(2,1)S(1)} %copy-done.1), custom_call_target="tpu_custom_call" | custom-call | bytes 5242880 | tf_op jit(solution)/shard_map/gather_window/pallas_call | solution.py:147
  99.0 0.0 copy-start.5
  99.0 16.9 %convolution_convert_fusion.k_ref.v_ref = bf16[2560,2048]{1,0:T(8,128)(2,1)} fusion(bf16[2560,1024]{1,0:T(8,128)(2,1)} %get-tuple-element.11, bf16[1024,3072]{1,0:T(8,128)(2,1)} %get-tuple-element.10), kind=kOutput, calls=%fused_computation.1 | convolution fusion | flops 10742661120 | bytes 19922944 | tf_op jit(solution)/shard_map/dot_general | solution.py:59
  115.9 0.0 copy-done.5
  115.9 23.4 %window_attention.1 = bf16[256,1024]{1,0:T(8,128)(2,1)} custom-call(bf16[256,1024]{1,0:T(8,128)(2,1)S(1)} %fusion.3.q_ref, bf16[2560,2048]{1,0:T(8,128)(2,1)} %convolution_convert_fusion.k_ref.v_ref, bf16[2560,2048]{1,0:T(8,128)(2,1)} %convolution_convert_fusion.k_ref.v_ref, bf16[1024,1024]{1,0:T(8,128)(2,1)S(1)} %get-tuple-element.12.out_w_ref, ...), custom_call_target="tpu_custom_call" | custom-call | flops 4831838208 | bytes 8388608 | tf_op jit(solution)/shard_map/window_attention/pallas_call | solution.py:440
  (2 shorter events, 0.0 us)
Async XLA Ops:
  5.0 1.9 %copy-start = (bf16[1024,1536]{1,0:T(8,128)(2,1)S(1)}, bf16[1024,1536]{1,0:T(8,128)(2,1)}, u32[]{:S(2)}) copy-start(bf16[1024,1536]{1,0:T(8,128)(2,1)} %shard_ref.2) | copy-start | bytes 9437188
  6.9 1.0 copy-start.2
  8.0 0.7 copy-start.3
  8.7 0.7 copy-start.4
  9.4 51.7 %copy-start.1 = (bf16[1024,512]{1,0:T(8,128)(2,1)S(1)}, bf16[1024,512]{1,0:T(8,128)(2,1)}, u32[]{:S(2)}) copy-start(bf16[1024,512]{1,0:T(8,128)(2,1)} %shard_ref.3) | copy-start | bytes 3145732
  99.0 16.9 %copy-start.5 = (f32[1024]{0:T(1024)S(1)}, f32[1024]{0:T(1024)}, u32[]{:S(2)}) copy-start(f32[1024]{0:T(1024)} %param.17) | copy-start | bytes 12292

commit v4 on v3

--- a/solution.py
+++ b/solution.py
@@ -52,13 +52,7 @@
         qkv_weight,
         slot_count,
     )
-    window, full_out = gather_window(conv_out, out_weight)
-    query = jnp.dot(
-        conv_out, full_qkv[:, :model_width], preferred_element_type=jnp.float32
-    ).astype(jnp.bfloat16)
-    key_value = jnp.dot(
-        window, full_qkv[:, model_width:], preferred_element_type=jnp.float32
-    ).astype(jnp.bfloat16)
+    query, key_value, full_out = gather_and_project(conv_out, full_qkv, out_weight)
     return attention(query, key_value, full_out, attn_gain[None, :], tok_rows, model_width)[None, :, :]
 
 
@@ -68,7 +62,8 @@
 
 
 def window_kernel(
-    count, conv_ref, shard_ref, win_ref, full_ref, send_sem, recv_sem, swap_sem, local_sem
+    count, conv_ref, weight_ref, shard_ref, query_ref, kv_ref, full_ref,
+    win_ref, held_weight, held_kv, send_sem, recv_sem, swap_sem, local_sem, weight_sem, kv_sem,
 ):
     me = lax.axis_index("seq")
     rows = conv_ref.shape[0]
@@ -84,6 +79,8 @@
         first = ((REACH_CHIPS - back) * 2 + core) * rows + chunk * part
         return win_ref.at[pl.ds(pl.multiple_of(first, part), part)]
 
+    load_weight = pltpu.make_async_copy(weight_ref, held_weight, weight_sem)
+    load_weight.start()
     own = pl.multiple_of((REACH_CHIPS * 2 + core) * rows, rows)
     win_ref[pl.ds(own, rows), :] = conv_ref[...]
 
@@ -113,59 +110,113 @@
     one = [message(2, j, 2 * odd, 1, beside) for j in chunks]
     three = [message(3, j, 2 + 2 * odd, 3, beside) for j in chunks]
     share = [[message(4 + back, j, back, back, twin) for j in chunks] for back in range(5)]
+    width = conv_ref.shape[1]
+    tile = 512
+    stores = []
+
+    def project(back, side):
+        first = pl.multiple_of(((REACH_CHIPS - back) * 2 + side) * rows, rows)
+        here = pl.ds(first, rows)
+
+        def columns(index, carry):
+            start = pl.multiple_of(index * tile, tile)
+            held_kv[here, pl.ds(start, tile)] = jnp.dot(
+                win_ref[here, :],
+                held_weight[:, pl.ds(pl.multiple_of(width + start, tile), tile)],
+                preferred_element_type=jnp.float32,
+            ).astype(jnp.bfloat16)
+            return carry
+
+        lax.fori_loop(0, 2 * width // tile, columns, 0)
+        store = pltpu.make_async_copy(held_kv.at[here], kv_ref.at[here], kv_sem.at[len(stores)])
+        store.start()
+        stores.append(store)
+
+    def shared(back):
+        for j in chunks:
+            share[back][j].wait_recv()
+        project(back, 1 - core)
+
     for j in chunks:
         two[j].start()
     for j in chunks:
         share[0][j].start()
+    load_weight.wait()
+    query_ref[...] = jnp.dot(
+        conv_ref[...], held_weight[:, :width], preferred_element_type=jnp.float32
+    ).astype(jnp.bfloat16)
     for j in chunks:
         two[j].wait_recv()
         four[j].start()
         one[j].start()
         share[2][j].start()
+        if j == 0:
+            project(0, core)
+        if j == 1:
+            shared(0)
     for j in chunks:
         four[j].wait_recv()
         three[j].start()
         share[4][j].start()
         one[j].wait_recv()
         share[1][j].start()
+        if j == 0:
+            project(2, core)
+        if j == 1:
+            shared(2)
     for j in chunks:
         three[j].wait_recv()
         share[3][j].start()
-    for back in range(5):
-        for j in chunks:
-            share[back][j].wait_recv()
+        if j == 0:
+            project(1, core)
+        if j == 1:
+            project(4, core)
+    shared(1)
+    project(3, core)
+    shared(4)
+    shared(3)
+    for store in stores:
+        store.wait()
     for group in [two, four, one, three] + share:
         for j in chunks:
             group[j].wait_send()
     swap.finish()
 
 
-def gather_window(conv_out, shard):
+def gather_and_project(conv_out, weight, shard):
     count = lax.axis_size("seq")
     rows, width = conv_out.shape
     slots = 2 * REACH_CHIPS + 2
     return pl.pallas_call(
         functools.partial(window_kernel, count),
         out_shape=[
-            jax.ShapeDtypeStruct((slots * rows, width), conv_out.dtype),
+            jax.ShapeDtypeStruct((rows, width), conv_out.dtype),
+            jax.ShapeDtypeStruct((slots * rows, 2 * width), conv_out.dtype),
             jax.ShapeDtypeStruct((shard.shape[0], 2 * shard.shape[1]), shard.dtype),
         ],
-        in_specs=[pl.BlockSpec(memory_space=pltpu.VMEM), pl.BlockSpec(memory_space=pl.ANY)],
-        out_specs=[pl.BlockSpec(memory_space=pltpu.VMEM), pl.BlockSpec(memory_space=pl.ANY)],
+        in_specs=[pl.BlockSpec(memory_space=pltpu.VMEM)] + [pl.BlockSpec(memory_space=pl.ANY)] * 2,
+        out_specs=[pl.BlockSpec(memory_space=pltpu.VMEM)] + [pl.BlockSpec(memory_space=pl.ANY)] * 2,
         scratch_shapes=[
+            pltpu.VMEM((slots * rows, width), conv_out.dtype),
+            pltpu.VMEM(weight.shape, weight.dtype),
+            pltpu.VMEM((slots * rows, 2 * width), conv_out.dtype),
             pltpu.SemaphoreType.DMA((9, CHUNKS)),
             pltpu.SemaphoreType.DMA((9, CHUNKS)),
             pltpu.SemaphoreType.DMA((4, 1)),
             pltpu.SemaphoreType.DMA,
+            pltpu.SemaphoreType.DMA,
+            pltpu.SemaphoreType.DMA((slots,)),
         ],
         compiler_params=pltpu.CompilerParams(
             collective_id=1, has_side_effects=True, vmem_limit_bytes=48 * 1024 * 1024
         ),
         cost_estimate=pl.CostEstimate(
-            flops=0, bytes_accessed=2 * slots * rows * width, transcendentals=0
+            flops=4 * slots * rows * width * width,
+            bytes_accessed=4 * slots * rows * width,
+            transcendentals=0,
         ),
-        name="gather_window",
-    )(conv_out, shard)
+        name="gather_and_project",
+    )(conv_out, weight, shard)
 
 
 LANES = 128

time: 140 us -> 125 us (0.89)
  matrix products: 19.2 us -> 0 us
  Pallas kernels: 111 us -> 115 us
    dot_general x2 -> x0, matrix products: 19.2 us -> none  [the longest x1 16.9 us: local(): jnp.dot(window, full_qkv[:, model_width:], preferred_element_type=jnp.flo...]
    pallas_call x1, Pallas kernels: 37.9 us -> 42.6 us  [gather_and_project(): pl.pallas_call(functools.partial(window_kernel, count), out_shape=[jax.Sh...]
where the time goes in v4:
time: 125 us
  Pallas kernels  115 us (92%)
  local copies, waits for them, and re-layouts  6.48 us (5%)
  other arithmetic  2.87 us (2%)
    pallas_call x1, Pallas kernels, embed_and_conv(): pl.pallas_call(functools.partial(embed_kernel, count, slots), out_shape=[...  49.3 us
    pallas_call x1, Pallas kernels, gather_and_project(): pl.pallas_call(functools.partial(window_kernel, count), out_shape=[jax.Sh...  42.6 us
    pallas_call x1, Pallas kernels, attention(): pl.pallas_call(functools.partial(attention_kernel, tok_rows), grid=(pairs...  23.4 us
    unnamed x12, local copies, waits for them, and re-layouts  4.34 us

profile of v4, /device:TPU:0, one launch (start us, length us, event | category | flops | bytes accessed | tf_op | source)
XLA Modules:
  0.0 124.7 jit_solution(14854172988482817479)
XLA Ops:
  0.0 0.7 multiply_bitcast_fusion
  0.7 0.7 fusion.4
  1.4 0.6 reduce-window.6
  1.9 0.2 slice_reduce_fusion
  2.2 0.8 fusion.3
  2.9 0.1 copy.12
  3.1 0.1 copy.11
  3.2 0.1 fusion
  3.3 1.6 %scatter_custom_fusion = s32[512]{0:T(512)S(1)} fusion(s32[256]{0:T(256)S(1)} %get-tuple-element.15, s32[256]{0:T(256)} %bitcast.36, s32[]{:T(128)} %constant.3.clone.1), kind=kCustom, calls=%fused_computation.13 | custom fusion | bytes 2560 | tf_op jit(solution)/shard_map/scatter | solution.py:44
  4.9 0.1 broadcast_in_dim.22.request_ref
  5.0 0.0 copy-start
  5.1 1.9 %copy-done = bf16[1024,1536]{1,0:T(8,128)(2,1)S(1)} copy-done((bf16[1024,1536]{1,0:T(8,128)(2,1)S(1)}, bf16[1024,1536]{1,0:T(8,128)(2,1)}, u32[]{:S(2)}) %copy-start) | copy-done | bytes 3145752
  6.9 0.0 copy-start.1
  6.9 1.0 copy-done.1
  8.0 0.0 copy-start.2
  8.0 0.7 copy-done.2
  8.7 0.0 copy-start.3
  8.7 0.7 copy-done.3
  9.4 0.0 copy-start.5
  9.4 49.3 %embed_and_conv.1 = (bf16[256,1024]{1,0:T(8,128)(2,1)S(1)}, bf16[1024,3072]{1,0:T(8,128)(2,1)}) custom-call(s32[512,128]{1,0:T(8,128)S(1)} %broadcast_in_dim.22.request_ref, s32[256,1]{1,0:T(8,128)S(1)} %get-tuple-element.16.slot_ref, bf16[256,1024]{1,0:T(8,128)(2,1)S(1)} %bitcast.30, bf16[2048,1024]{1,0:T(8,128)(2,1)} %table_ref.1, f32[1,1024]{1,0:T(1,128)S(1)} %bitcast.31, ...), custom_call_target="tpu_custom_call" | custom-call | flops 2147483648 | bytes 4194304 | tf_op jit(solution)/shard_map/embed_and_conv/pallas_call | solution.py:396
  58.7 0.0 copy-done.5
  58.7 0.0 copy-start.4
  58.8 42.6 %gather_and_project.1 = (bf16[256,1024]{1,0:T(8,128)(2,1)S(1)}, bf16[2560,2048]{1,0:T(8,128)(2,1)}, bf16[1024,1024]{1,0:T(8,128)(2,1)S(1)}) custom-call(bf16[256,1024]{1,0:T(8,128)(2,1)S(1)} %get-tuple-element.10.conv_ref, bf16[1024,3072]{1,0:T(8,128)(2,1)} %get-tuple-element.11.weight_ref, bf16[1024,512]{1,0:T(8,128)(2,1)S(1)} %copy-done.5), custom_call_target="tpu_custom_call" | custom-call | flops 10737418240 | bytes 10485760 | tf_op jit(solution)/shard_map/gather_and_project/pallas_call | solution.py:190
  101.3 0.0 copy-done.4
  101.4 23.4 %window_attention.1 = bf16[256,1024]{1,0:T(8,128)(2,1)} custom-call(bf16[256,1024]{1,0:T(8,128)(2,1)S(1)} %get-tuple-element.12.q_ref, bf16[2560,2048]{1,0:T(8,128)(2,1)} %get-tuple-element.13.k_ref.v_ref, bf16[2560,2048]{1,0:T(8,128)(2,1)} %get-tuple-element.13.k_ref.v_ref, bf16[1024,1024]{1,0:T(8,128)(2,1)S(1)} %get-tuple-element.14.out_w_ref, ...), custom_call_target="tpu_custom_call" | custom-call | flops 4831838208 | bytes 8388608 | tf_op jit(solution)/shard_map/window_attention/pallas_call | solution.py:491
  (2 shorter events, 0.0 us)
Async XLA Ops:
  5.0 1.9 %copy-start = (bf16[1024,1536]{1,0:T(8,128)(2,1)S(1)}, bf16[1024,1536]{1,0:T(8,128)(2,1)}, u32[]{:S(2)}) copy-start(bf16[1024,1536]{1,0:T(8,128)(2,1)} %shard_ref.2) | copy-start | bytes 9437188
  6.9 1.0 copy-start.1
  8.0 0.7 copy-start.2
  8.7 0.7 copy-start.3
  9.4 49.4 %copy-start.5 = (bf16[1024,512]{1,0:T(8,128)(2,1)S(1)}, bf16[1024,512]{1,0:T(8,128)(2,1)}, u32[]{:S(2)}) copy-start(bf16[1024,512]{1,0:T(8,128)(2,1)} %shard_ref.3) | copy-start | bytes 3145732
  58.7 42.6 %copy-start.4 = (f32[1024]{0:T(1024)S(1)}, f32[1024]{0:T(1024)}, u32[]{:S(2)}) copy-start(f32[1024]{0:T(1024)} %param.17) | copy-start | bytes 12292
